TPU v7x, 32 devices: a whole 2x2x4 slice. The times are simulated.
32 devices in a mesh: row: 16 (over z, y, core), col: 2 (over x).
Axes of the slice: x: 2, y: 2, z: 4, core: 2. Of those that a mesh axis runs over, the one named last changes fastest.
Arguments:
- left_blocks: bfloat16 [2, 2, 64, 4096], P('col', None, 'row'), may hold values from -0.75 to 0.75
- left_slots: int32 [2, 2, 64], P('col', None, 'row'), may hold values from 0 to 15, as said below
- left_lengths: int32 [2, 2, 8], P('col'), may hold values from 1 to 8, as said below
- right_blocks: bfloat16 [2, 16, 32, 4096], P('col', 'row'), may hold values from -6 to 6
- right_places: int32 [2, 16, 32], P('col', 'row'), may hold values from 0 to 255, as said below
- right_count: int32 [2, 16], P('col', 'row'), may hold values from 1 to 32, as said below
Outputs:
- product: float32 [1024, 16384], P('col', 'row')
Inputs may be any that keep to these rules, and one draw needn't show every extreme that they name: `left_slots`: within one block-row of one left tile the 8 slots name distinct block-columns. `left_lengths`: some block-row of some left tile has all 8 slots live. `right_places`: within one right tile the 32 slots name distinct places. `right_count`: some right tile has all 32 slots live.
All inputs are finite; a program needn't handle non-finite values.
Results may differ from a plain program's by a relative error of at most 0.0003.
Values may be sent and summed in bfloat16 or wider, within the bound.
No kernel may reach another device: no remote copies, remote signals or barrier semaphores. Data moves between devices by JAX's collectives and lax.ppermute only.
A program may use at most 192 MiB of HBM per device.

v0:
```python
import math

import jax
import jax.numpy as jnp
from jax import lax
from jax.sharding import PartitionSpec as P

KB = 16
BCR = 16


def shifted(x, axis, by):
    peers = lax.axis_size(axis)
    return lax.ppermute(x, axis, [(i, (i + by) % peers) for i in range(peers)])


def select(stacked, chosen):
    return lax.dynamic_index_in_dim(stacked, chosen, 0, keepdims=False)


def densify(values, places, live_count):
    slot_count = values.shape[0]
    block_side = math.isqrt(values.shape[1])
    live_mask = jnp.arange(slot_count, dtype=jnp.int32) < live_count
    target = (
        jnp.arange(KB, dtype=jnp.int32)[:, None] * BCR + jnp.arange(BCR, dtype=jnp.int32)[None, :]
    )
    hits = (places[:, None, None] == target[None, :, :]) & live_mask[:, None, None]
    hits = hits.astype(values.dtype)
    blocks = values.reshape(slot_count, block_side, block_side)
    dense_tile = jnp.einsum("skj,sab->kajb", hits, blocks, preferred_element_type=jnp.float32)
    return dense_tile.astype(values.dtype).reshape(KB * block_side, BCR * block_side)


def contribute(running, tile_vals, tile_cols, lengths, dense_right):
    row_count = lengths.shape[0]
    per_row = tile_cols.shape[0] // row_count
    block_side = math.isqrt(tile_vals.shape[1])
    position = jnp.arange(per_row, dtype=jnp.int32)
    live_mask = position[None, :] < lengths[:, None]
    columns = tile_cols.reshape(row_count, per_row)
    hits = (columns[:, :, None] == jnp.arange(KB, dtype=jnp.int32)[None, None, :]) & live_mask[
        :, :, None
    ]
    hits = hits.astype(tile_vals.dtype)
    blocks = tile_vals.reshape(row_count, per_row, block_side, block_side)
    dense_left = jnp.einsum("ipk,ipxa->ixka", hits, blocks, preferred_element_type=jnp.float32)
    dense_left = dense_left.astype(tile_vals.dtype).reshape(row_count * block_side, KB * block_side)
    return running + jnp.dot(dense_left, dense_right, preferred_element_type=jnp.float32)


def shards(left_blocks, left_slots, left_lengths, right_blocks, right_places, right_count):
    col_count = lax.axis_size("col")
    col_index = lax.axis_index("col")
    left_vals = left_blocks[0]
    left_cols = left_slots[0]
    row_lengths = left_lengths[0]
    block_side = math.isqrt(left_blocks.shape[-1])
    running = jnp.zeros((row_lengths.shape[1] * block_side, BCR * block_side), jnp.float32)
    right_vals = right_blocks[0, 0]
    right_spots = right_places[0, 0]
    right_live = right_count[0]
    held_vals, held_spots, held_live = (right_vals, right_spots, right_live)
    for turn_index in range(col_count):
        group = (col_index - turn_index) % col_count
        tile_vals = lax.all_gather(select(left_vals, group), "row", axis=0, tiled=True)
        tile_cols = lax.all_gather(select(left_cols, group), "row", axis=0, tiled=True)
        dense_tile = densify(held_vals, held_spots, held_live[0])
        running = contribute(running, tile_vals, tile_cols, select(row_lengths, group), dense_tile)
        if turn_index + 1 < col_count:
            held_vals, held_spots, held_live = shifted((held_vals, held_spots, held_live), "col", 1)
    return running


def solution(mesh):
    return jax.shard_map(
        shards,
        mesh=mesh,
        in_specs=(
            P("col", None, "row", None),
            P("col", None, "row"),
            P("col", None, None),
            P("col", "row", None, None),
            P("col", "row", None),
            P("col", "row"),
        ),
        out_specs=P("col", "row"),
        check_vma=False,
    )
```

profile of v0, /device:TPU:1, one launch (start us, length us, event | category | flops | bytes accessed | tf_op | source)
XLA Modules:
  0.0 110.9 jit_solution(1145495825308761509)
XLA Ops:
  0.0 2.0 %collective-permute-start = (s32[32]{0:T(128)}, s32[32]{0:T(128)S(1)}, u32[]{:S(2)}, u32[]{:S(2)}) collective-permute-start(s32[32]{0:T(128)} %bitcast.68), channel_id=1, source_target_pairs={{0,1},{1,0},{2,3},{3,2},{4,5},{5,4},{6,7},{7,6},{8,9},{9,8},{10,11... | collective-permute-start | bytes 392 | tf_op jit(solution)/shard_map/ppermute | solution.py:14
  2.0 0.0 collective-permute-start.2
  2.1 1.4 %collective-permute-start.1 = (s32[1]{0:T(128)}, s32[1]{0:T(128)}, u32[]{:S(2)}, u32[]{:S(2)}) collective-permute-start(s32[1]{0:T(128)} %bitcast.17), channel_id=1, source_target_pairs={{0,1},{1,0},{2,3},{3,2},{4,5},{5,4},{6,7},{7,6},{8,9},{9,8},{10,11... | collective-permute-start | bytes 20 | tf_op jit(solution)/shard_map/ppermute | solution.py:14
  3.5 2.3 %reshape_squeeze.3 = bf16[32,64,64]{2,1,0:T(8,128)(2,1)} reshape(bf16[1,1,32,4096]{3,2,1,0:T(8,128)(2,1)} %param.9) | data formatting | bytes 524288 | tf_op jit(solution)/shard_map/reshape;squeeze | solution.py:30
  6.5 0.8 constant_dynamic-slice_fusion.2
  7.3 0.1 copy.22
  7.3 0.0 copy-start.4
  7.3 0.0 copy-start.2
  7.4 0.0 copy-start.1
  7.4 25.9 %all-gather = bf16[1,1,64,4096]{3,1,0,2:T(2,128)(2,1)S(1)} all-gather(bf16[1,1,4,4096]{3,1,0,2:T(2,128)(2,1)S(1)} %copy.22), channel_id=2, replica_groups=mesh['row'=16,'col'=2] {'row'}, dimensions={2}, use_global_device_ids=true | all-gather | bytes 557056 | tf_op jit(solution)/shard_map/all_gather | solution.py:66
  33.3 3.1 %reduce = bf16[64,4096]{1,0:T(8,128)(2,1)S(1)} reduce(bf16[1,1,64,4096]{3,1,0,2:T(2,128)(2,1)S(1)} %all-gather, bf16[]{:T(256)} %constant.68), dimensions={0,1}, to_apply=%all-gather.reduce_sub_computation | reduce | bytes 1048578 | tf_op jit(solution)/shard_map/all_gather | solution.py:66
  36.4 1.1 %reshape.119 = bf16[8,8,64,64]{3,2,1,0:T(8,128)(2,1)S(1)} reshape(bf16[64,4096]{1,0:T(8,128)(2,1)S(1)} %reduce) | data formatting | bytes 1048576 | tf_op jit(solution)/shard_map/reshape | solution.py:46
  37.6 0.0 copy-done.4
  37.6 0.6 dynamic-slice.6
  38.8 0.0 copy-done.2
  38.8 0.1 fusion.29
  38.9 0.1 fusion.32
  39.0 4.6 %all-reduce.2 = (s32[64]{0:T(128)S(1)}, s32[64]{0:T(128)S(1)}) all-reduce(s32[64]{0:T(128)S(1)} %fusion.29, s32[64]{0:T(128)S(1)} %fusion.32), channel_id=3, replica_groups=mesh['row'=16,'col'=2] {'row'}, use_global_device_ids=true, to_apply=%add | all-reduce | flops 128 | bytes 1024
  43.6 0.1 eq.61
  43.7 0.0 copy-done.1
  43.7 0.1 iota_compare_fusion.3
  43.8 1.2 %convert_bitcast_fusion.3 = bf16[8,64,16,64]{3,2,1,0:T(8,128)(2,1)S(1)} fusion(bf16[8,8,64,64]{3,2,1,0:T(8,128)(2,1)S(1)} %reshape.119, s32[8,8]{1,0:T(8,128)S(1)} %eq.61, pred[8,8]{1,0:T(8,128)(4,1)S(1)} %iota_compare_fusion.3), kind=kOutput, calls=%fused_computation.3 | convolution fusion | flops 8914944 | bytes 1573184 | tf_op jit(solution)/shard_map/ipk,ipxa->ixka/dot_general | solution.py:47
  45.0 0.0 copy-start
  45.0 0.0 copy-start.3
  45.0 2.3 %reshape.120 = bf16[512,1024]{1,0:T(8,128)(2,1)} reshape(bf16[8,64,16,64]{3,2,1,0:T(8,128)(2,1)S(1)} %convert_bitcast_fusion.3) | data formatting | bytes 2097152 | tf_op jit(solution)/shard_map/reshape | solution.py:48
  47.3 0.1 iota_add_fusion
  47.4 0.0 copy-done
  47.4 0.0 copy-done.3
  47.4 3.2 %convert_bitcast_fusion.1 = bf16[16,64,16,64]{3,2,1,0:T(8,128)(2,1)} fusion(bf16[32,64,64]{2,1,0:T(8,128)(2,1)S(1)} %copy-done, s32[16,16]{1,0:T(8,128)S(1)} %iota_add_fusion, s32[32]{0:T(128)S(1)} %bitcast.69, pred[32]{0:T(512)(128)(4,1)S(1)} %iota_compare_fusion.5), kind=kOutput, calls=%fused_computation.1 | convolution fusion | flops 68173824 | bytes 2360480 | tf_op jit(solution)/shard_map/skj,sab->kajb/dot_general | solution.py:31
  50.6 5.5 %reshape.121 = bf16[1024,1024]{1,0:T(8,128)(2,1)S(1)} reshape(bf16[16,64,16,64]{3,2,1,0:T(8,128)(2,1)} %convert_bitcast_fusion.1) | data formatting | bytes 4194304 | tf_op jit(solution)/shard_map/reshape | solution.py:32
  56.1 0.1 copy.23
  56.1 28.1 %all-gather.2 = bf16[1,1,64,4096]{3,1,0,2:T(2,128)(2,1)S(1)} all-gather(bf16[1,1,4,4096]{3,1,0,2:T(2,128)(2,1)S(1)} %copy.23), channel_id=4, replica_groups=mesh['row'=16,'col'=2] {'row'}, dimensions={2}, use_global_device_ids=true | all-gather | bytes 557056 | tf_op jit(solution)/shard_map/all_gather | solution.py:66
  84.3 3.9 %reduce.1 = bf16[64,4096]{1,0:T(8,128)(2,1)} reduce(bf16[1,1,64,4096]{3,1,0,2:T(2,128)(2,1)S(1)} %all-gather.2, bf16[]{:T(256)} %constant.68), dimensions={0,1}, to_apply=%all-gather.2.reduce_sub_computation | reduce | bytes 1048578 | tf_op jit(solution)/shard_map/all_gather | solution.py:66
  88.2 2.1 %reshape.122 = bf16[8,8,64,64]{3,2,1,0:T(8,128)(2,1)S(1)} reshape(bf16[64,4096]{1,0:T(8,128)(2,1)} %reduce.1) | data formatting | bytes 1048576 | tf_op jit(solution)/shard_map/reshape | solution.py:46
  90.3 0.1 eq.69
  90.3 0.1 iota_compare_fusion.2
  90.4 3.8 %fusion.34 = f32[512,1024]{1,0:T(8,128)} fusion(bf16[512,1024]{1,0:T(8,128)(2,1)} %reshape.120, bf16[1024,1024]{1,0:T(8,128)(2,1)S(1)} %reshape.121), kind=kOutput, calls=%fused_computation.51 | convolution fusion | flops 1073741824 | bytes 5242880 | tf_op jit(solution)/shard_map/dot_general | solution.py:49
  94.2 1.2 %convert_bitcast_fusion.2 = bf16[8,64,16,64]{3,2,1,0:T(8,128)(2,1)S(1)} fusion(bf16[8,8,64,64]{3,2,1,0:T(8,128)(2,1)S(1)} %reshape.122, s32[8,8]{1,0:T(8,128)S(1)} %eq.69, pred[8,8]{1,0:T(8,128)(4,1)S(1)} %iota_compare_fusion.2), kind=kOutput, calls=%fused_computation.2 | convolution fusion | flops 8914944 | bytes 1573184 | tf_op jit(solution)/shard_map/ipk,ipxa->ixka/dot_general | solution.py:47
  95.4 1.5 %reshape.123 = bf16[512,1024]{1,0:T(8,128)(2,1)S(1)} reshape(bf16[8,64,16,64]{3,2,1,0:T(8,128)(2,1)S(1)} %convert_bitcast_fusion.2) | data formatting | bytes 2097152 | tf_op jit(solution)/shard_map/reshape | solution.py:48
  96.9 0.0 collective-permute-done.1
  96.9 0.6 iota_compare_fusion.4
  97.5 0.0 collective-permute-done.2
  97.5 0.5 reshape.124
  98.0 0.0 collective-permute-done
  98.0 3.2 %convert_bitcast_fusion = bf16[16,64,16,64]{3,2,1,0:T(8,128)(2,1)} fusion(bf16[32,64,64]{2,1,0:T(8,128)(2,1)S(1)} %reshape.124, s32[32]{0:T(128)S(1)} %collective-permute-done, s32[16,16]{1,0:T(8,128)S(1)} %iota_add_fusion, pred[32]{0:T(512)(128)(4,1)S(1)} %iota_compare_fusion.4), kind=kOutput, calls=%fused_computation | convolution fusion | flops 68173824 | bytes 2360480 | tf_op jit(solution)/shard_map/skj,sab->kajb/dot_general | solution.py:31
  101.3 5.5 %reshape.125 = bf16[1024,1024]{1,0:T(8,128)(2,1)S(1)} reshape(bf16[16,64,16,64]{3,2,1,0:T(8,128)(2,1)} %convert_bitcast_fusion) | data formatting | bytes 4194304 | tf_op jit(solution)/shard_map/reshape | solution.py:32
  106.7 4.2 %convolution_add_fusion = f32[512,1024]{1,0:T(8,128)} fusion(f32[512,1024]{1,0:T(8,128)} %fusion.34, bf16[512,1024]{1,0:T(8,128)(2,1)S(1)} %reshape.123, bf16[1024,1024]{1,0:T(8,128)(2,1)S(1)} %reshape.125), kind=kOutput, calls=%fused_computation.4 | convolution fusion | flops 1074266112 | bytes 7340032 | tf_op jit(solution)/shard_map/dot_general | solution.py:49
  (5 shorter events, 0.0 us)
Async XLA Ops:
  0.0 98.0 %collective-permute-start = (s32[32]{0:T(128)}, s32[32]{0:T(128)S(1)}, u32[]{:S(2)}, u32[]{:S(2)}) collective-permute-start(s32[32]{0:T(128)} %bitcast.68), channel_id=1, source_target_pairs={{0,1},{1,0},{2,3},{3,2},{4,5},{5,4},{6,7},{7,6},{8,9},{9,8},{10,11... | collective-permute-start | bytes 392 | tf_op jit(solution)/shard_map/ppermute | solution.py:14
  2.0 95.4 %collective-permute-start.2 = (bf16[32,4096]{1,0:T(8,128)(2,1)}, bf16[32,4096]{1,0:T(8,128)(2,1)S(1)}, u32[]{:S(2)}, u32[]{:S(2)}) collective-permute-start(bf16[32,4096]{1,0:T(8,128)(2,1)} %bitcast.67), channel_id=1, source_target_pairs={{0,1},{1,0},{2,3},{3,2},{4,5},{5,4},{6,7},{7,6},{8,9},{9,8},{10,11... | collective-permute-start | bytes 786440 | tf_op jit(solution)/shard_map/ppermute | solution.py:14
  2.1 94.8 %collective-permute-start.1 = (s32[1]{0:T(128)}, s32[1]{0:T(128)}, u32[]{:S(2)}, u32[]{:S(2)}) collective-permute-start(s32[1]{0:T(128)} %bitcast.17), channel_id=1, source_target_pairs={{0,1},{1,0},{2,3},{3,2},{4,5},{5,4},{6,7},{7,6},{8,9},{9,8},{10,11... | collective-permute-start | bytes 20 | tf_op jit(solution)/shard_map/ppermute | solution.py:14
  7.3 30.2 %copy-start.4 = (u32[32]{0:T(128)S(1)}, u32[32]{0:T(128)}, u32[]{:S(2)}) copy-start(u32[32]{0:T(128)} %constant.58) | copy-start | bytes 388
  7.3 31.5 %copy-start.2 = (s32[1,2,4]{2,1,0:T(2,128)S(1)}, s32[1,2,4]{2,1,0:T(2,128)}, u32[]{:S(2)}) copy-start(s32[1,2,4]{2,1,0:T(2,128)} %param.7) | copy-start | bytes 100
  7.4 36.3 %copy-start.1 = (s32[1,2,8]{2,1,0:T(2,128)S(1)}, s32[1,2,8]{2,1,0:T(2,128)}, u32[]{:S(2)}) copy-start(s32[1,2,8]{2,1,0:T(2,128)} %param.8) | copy-start | bytes 196
  45.0 2.4 %copy-start = (bf16[32,64,64]{2,1,0:T(8,128)(2,1)S(1)}, bf16[32,64,64]{2,1,0:T(8,128)(2,1)}, u32[]{:S(2)}) copy-start(bf16[32,64,64]{2,1,0:T(8,128)(2,1)} %reshape_squeeze.3) | copy-start | bytes 786436
  45.0 2.4 %copy-start.3 = (s32[1,1,32]{2,1,0:T(1,128)S(1)}, s32[1,1,32]{2,1,0:T(1,128)}, u32[]{:S(2)}) copy-start(s32[1,1,32]{2,1,0:T(1,128)} %param.10) | copy-start | bytes 388
where the time goes:
time: 112 us; the launch traced here: 111 us
  blocking collectives  58.6 us (52%)
  local copies, waits for them, and re-layouts  22.6 us (20%)
  matrix products  16.8 us (15%)
  other arithmetic  7.88 us (7%)
  starting transfers between devices  3.51 us (3%)
  between operations  1.52 us (1%)
    all_gather x2, blocking collectives, shards(): lax.all_gather(select(left_vals, group), 'row', axis=0, tiled=True)  54 us
    reshape x2, local copies, waits for them, and re-layouts, densify(): dense_tile.astype(values.dtype).reshape(KB * block_side, BCR * block_side)  10.9 us
    dot_general x2, matrix products, contribute(): jnp.dot(dense_left, dense_right, preferred_element_type=jnp.float32)  7.97 us
    all_gather x2, other arithmetic, shards(): lax.all_gather(select(left_vals, group), 'row', axis=0, tiled=True)  7.09 us
    dot_general x2, matrix products, densify(): jnp.einsum('skj,sab->kajb', hits, blocks, preferred_element_type=jnp.floa...  6.47 us
    unnamed x1, blocking collectives  4.57 us
    reshape x2, local copies, waits for them, and re-layouts, contribute(): dense_left.astype(tile_vals.dtype)  3.79 us
    ppermute x3, starting transfers between devices, shifted(): return lax.ppermute(x, axis, [(i, (i + by) % peers) for i in range(peers)])  3.51 us
  transfers between devices with their start and end apart: 3, of which 0 were waited for; matrix products, arithmetic and copies ran while one was open for 31% of the time, Pallas kernels for 0%

commit v1 on v0

v1 whole, which is shorter than its diff:
```python
import functools
import math

import jax
import jax.numpy as jnp
from jax import lax
from jax.experimental import pallas as pl
from jax.experimental.pallas import tpu as pltpu
from jax.sharding import PartitionSpec as P

KB = 16
BCR = 16
LANES = 128
META = 16


def swapped(x, mask):
    peers = lax.axis_size("row")
    return lax.ppermute(x, "row", [(i, i ^ mask) for i in range(peers)])


def low_half(rows):
    return lax.broadcasted_iota(jnp.int32, (rows, LANES), 1) < LANES // 2


def pack_kernel(where_ref, slots_ref, lengths_ref, left_ref, out_ref, tall, square):
    tiles, own, _ = left_ref.shape
    block_rows = lengths_ref.shape[1]
    per_row = where_ref[1]
    first = where_ref[0] * own
    row = lax.div(first, per_row)
    place = lax.rem(first, per_row)
    low = low_half(32)
    low_meta = low_half(META)
    meta_row = lax.broadcasted_iota(jnp.int32, (META, LANES), 0)
    meta = jnp.full((META, LANES), -1.0, jnp.float32)
    at = 0
    for m in range(tiles):
        values = left_ref[m].astype(jnp.float32)
        for t in range(32):
            tall[pl.ds(t * 8, own), :] = values[:, t * LANES : (t + 1) * LANES]
        live = lengths_ref[m, row]
        for s in range(0, own, 2):
            one = tall[pl.ds(s, 32, stride=8), :]
            two = tall[pl.ds(s + 1, 32, stride=8), :]
            even = jnp.where(low, one, pltpu.roll(two, LANES // 2, 1))
            odd = jnp.where(low, pltpu.roll(one, LANES // 2, 1), two)
            square[pl.ds(0, 32, stride=2), :] = even
            square[pl.ds(1, 32, stride=2), :] = odd
            out_ref[at * 64 : at * 64 + 64, :] = square[...].astype(out_ref.dtype)
            a = jnp.where(place + s < live, slots_ref[m, s], -1).astype(jnp.float32)
            b = jnp.where(place + s + 1 < live, slots_ref[m, s + 1], -1).astype(jnp.float32)
            meta = jnp.where(meta_row == at, jnp.where(low_meta, a, b), meta)
            at += 1
    out_ref[at * 64 : at * 64 + META, :] = meta.astype(out_ref.dtype)


def pack(left, slots, lengths, per_row):
    tiles, own, _ = left.shape
    where = jnp.stack([lax.axis_index("row").astype(jnp.int32), jnp.int32(per_row)])
    rows = tiles * own // 2 * 64 + META
    return pl.pallas_call(
        pack_kernel,
        out_shape=jax.ShapeDtypeStruct((rows, LANES), left.dtype),
        in_specs=[pl.BlockSpec(memory_space=pltpu.SMEM)] * 3 + [pl.BlockSpec(memory_space=pltpu.VMEM)],
        out_specs=pl.BlockSpec(memory_space=pltpu.VMEM),
        scratch_shapes=[pltpu.VMEM((256, LANES), jnp.float32), pltpu.VMEM((64, LANES), jnp.float32)],
    )(where, slots, lengths, left)


def repeat(count, body):
    if count <= 2:
        for i in range(count):
            body(i)
    else:
        pl.loop(0, count)(body)


def place_right(values_ref, places_ref, count_ref, dense_ref, base, tall, square):
    slots = values_ref.shape[0]
    half = lax.broadcasted_iota(jnp.int32, (32, LANES), 1) // (LANES // 2)
    count = count_ref[0, 0]

    def some(g):
        values = values_ref[pl.ds(g * 16, 16), :].astype(jnp.float32)
        for t in range(32):
            tall[pl.ds(t * 16, 16), :] = values[:, t * LANES : (t + 1) * LANES]
        for s in range(16):
            spot = places_ref[0, g * 16 + s]
            live = g * 16 + s < count
            k, j = lax.shift_right_logical(spot, 4), lax.bitwise_and(spot, 15)
            side = lax.bitwise_and(j, 1)
            plain = tall[pl.ds(s, 32, stride=16), :]
            turned = pltpu.roll(plain, LANES // 2, 1)
            keep = half == jnp.where(live, side, -1)
            even = jnp.where(keep, jnp.where(side == 0, plain, turned), 0.0)
            odd = jnp.where(keep, jnp.where(side == 0, turned, plain), 0.0)
            y = square.at[s % square.shape[0]]
            y[pl.ds(0, 32, stride=2), :] = even
            y[pl.ds(1, 32, stride=2), :] = odd
            at = (
                pl.ds(pl.multiple_of(base + k * 64, 64), 64),
                pl.ds(pl.multiple_of(lax.shift_right_logical(j, 1) * LANES, LANES), LANES),
            )
            dense_ref[at] = dense_ref[at] + y[...].astype(dense_ref.dtype)

    repeat(slots // 16, some)


def place_left(parcels, row, tiles, pairs, dense_ref, names_ref):
    half = (lax.broadcasted_iota(jnp.int32, (16, LANES), 1) // (LANES // 2)).astype(jnp.float32)
    body = tiles * pairs * 64
    for i, parcel in enumerate(parcels):
        names_ref[i * META : i * META + META, :] = parcel[body : body + META, :].astype(jnp.float32)

    def one(m):
        names = []
        for i, parcel in enumerate(parcels):
            for p in range(pairs):
                at = m * pairs + p
                name = jnp.broadcast_to(names_ref[pl.ds(i * META + at, 1), :], (16, LANES))
                turned = pltpu.roll(name, LANES // 2, 1)
                names.append((parcel, at * 64, (name - half).astype(jnp.bfloat16), (turned - half).astype(jnp.bfloat16)))
        for c in range(4):
            blocks = []
            for parcel, start, a, b in names:
                v = parcel[pl.ds(start + c * 16, 16), :]
                w = pltpu.roll(v.astype(jnp.float32), LANES // 2, 1).astype(v.dtype)
                blocks.append((v, w, a, b))
            for t in range(KB // 2):
                want = jnp.bfloat16(2 * t)
                acc = jnp.zeros((16, LANES), dense_ref.dtype)
                for v, w, a, b in blocks:
                    acc = jnp.where(a == want, v, acc)
                    acc = jnp.where(b == want, w, acc)
                dense_ref[
                    pl.ds(pl.multiple_of(row * 64 + c * 16, 16), 16),
                    pl.ds(pl.multiple_of(m * KB * 64 + t * LANES, LANES), LANES),
                ] = acc

    repeat(tiles, one)


def product_kernel(tiles, pairs, masks, per_row, *refs):
    where_ref = refs[0]
    refs = refs[1:]
    places, refs = refs[:tiles], refs[tiles:]
    counts, refs = refs[:tiles], refs[tiles:]
    rights, refs = refs[:tiles], refs[tiles:]
    parcels, refs = dict(zip(masks, refs[: len(masks)])), refs[len(masks) :]
    out_ref, left_dense, right_dense, result, tall, square, names, sems = refs
    me = where_ref[0]
    first = where_ref[1]
    right_dense[...] = jnp.zeros_like(right_dense)
    for m in range(tiles):
        group = lax.rem(first - m + tiles, tiles)
        place_right(rights[m], places[m], counts[m], right_dense, group * KB * 64, tall, square)
    sharing = per_row // (2 * pairs)
    for base in range(0, len(masks), sharing):
        row = lax.div(lax.bitwise_xor(me, base), sharing)
        place_left([parcels[base + i] for i in range(sharing)], row, tiles, pairs, left_dense, names)
    width = 256
    copies = []
    for n in range(out_ref.shape[1] // width):
        span = slice(n * width, n * width + width)
        if tiles <= 2:
            result[:, span] = jnp.dot(left_dense[...], right_dense[:, span], preferred_element_type=jnp.float32)
        else:
            result[:, span] = jnp.zeros_like(result[:, span])

            @pl.loop(0, tiles)
            def _(m, span=span):
                part = pl.ds(pl.multiple_of(m * KB * 64, KB * 64), KB * 64)
                result[:, span] += jnp.dot(left_dense[:, part], right_dense[part, span], preferred_element_type=jnp.float32)

        copy = pltpu.make_async_copy(result.at[:, span], out_ref.at[:, span], sems.at[n])
        copy.start()
        copies.append(copy)
    for copy in copies:
        copy.wait()


def shards(left_blocks, left_slots, left_lengths, right_blocks, right_places, right_count):
    peers = lax.axis_size("row")
    cols = lax.axis_size("col")
    tiles, own = left_blocks.shape[1], left_blocks.shape[2]
    block_rows = left_lengths.shape[2]
    per_row = peers * own // block_rows
    pairs = own // 2
    side = math.isqrt(left_blocks.shape[-1])

    def from_col(x, by):
        return x if by == 0 else lax.ppermute(x, "col", [(i, (i + by) % cols) for i in range(cols)])

    rights, places, counts = [], [], []
    for by in range(cols):
        places.append(from_col(right_places[0], by))
        counts.append(from_col(right_count, by))
        rights.append(from_col(right_blocks[0, 0], by))
    parcel = pack(left_blocks[0], left_slots[0], left_lengths[0], per_row)
    held = {0: parcel}
    for mask in range(4, peers, 4):
        held[mask] = swapped(parcel, mask)
    for mask in range(0, peers, 4):
        held[mask + 2] = swapped(held[mask], 2)
    for mask in range(0, peers, 2):
        held[mask + 1] = swapped(held[mask], 1)
    masks = list(range(peers))
    where = jnp.stack([lax.axis_index("row").astype(jnp.int32), lax.axis_index("col").astype(jnp.int32)])
    height, depth, width = block_rows * side, tiles * KB * side, BCR * side
    smem, vmem = pl.BlockSpec(memory_space=pltpu.SMEM), pl.BlockSpec(memory_space=pltpu.VMEM)
    return pl.pallas_call(
        functools.partial(product_kernel, tiles, pairs, masks, per_row),
        out_shape=jax.ShapeDtypeStruct((height, width), jnp.float32),
        in_specs=[smem] * (1 + 2 * tiles) + [vmem] * (tiles + peers),
        out_specs=pl.BlockSpec(memory_space=pltpu.HBM),
        scratch_shapes=[
            pltpu.VMEM((height, depth), left_blocks.dtype),
            pltpu.VMEM((depth, width), left_blocks.dtype),
            pltpu.VMEM((height, width), jnp.float32),
            pltpu.VMEM((512, LANES), jnp.float32),
            pltpu.VMEM((4, side, LANES), jnp.float32),
            pltpu.VMEM((per_row // own * META, LANES), jnp.float32),
            pltpu.SemaphoreType.DMA((width // 256,)),
        ],
        compiler_params=pltpu.CompilerParams(vmem_limit_bytes=40 * 1024 * 1024),
    )(where, *places, *counts, *rights, *[held[m] for m in masks])


def solution(mesh):
    return jax.shard_map(
        shards,
        mesh=mesh,
        in_specs=(
            P("col", None, "row", None),
            P("col", None, "row"),
            P("col", None, None),
            P("col", "row", None, None),
            P("col", "row", None),
            P("col", "row"),
        ),
        out_specs=P("col", "row"),
        check_vma=False,
    )
```

time: 112 us -> 42.2 us (0.38)
  blocking collectives: 58.6 us -> 0 us
  local copies, waits for them, and re-layouts: 22.6 us -> 2.49 us
  matrix products: 16.8 us -> 0 us
  starting transfers between devices: 3.51 us -> 19.7 us
  waiting for transfers between devices: 0.01 us -> 9.22 us
  Pallas kernels: 0 us -> 8.98 us
  other arithmetic: 7.88 us -> 0.67 us
    all_gather x2 -> x0, blocking collectives: 54 us -> none  [shards(): lax.all_gather(select(left_vals, group), 'row', axis=0, tiled=True)]
    reshape x7 -> x0, local copies, waits for them, and re-layouts: 18.4 us -> none  [the longest x2 10.9 us: densify(): dense_tile.astype(values.dtype).reshape(KB * block_side, BCR * block_side)]
    dot_general x6 -> x0, matrix products: 16.8 us -> none  [the longest x2 7.97 us: contribute(): jnp.dot(dense_left, dense_right, preferred_element_type=jnp.float32)]
    ppermute x3 -> x18, starting transfers between devices: 3.51 us -> 19.7 us  [the longest x15 17.3 us: swapped(): return lax.ppermute(x, 'row', [(i, i ^ mask) for i in range(peers)])]
    ppermute x3 -> x18, waiting for transfers between devices: 0.01 us -> 9.22 us  [the longest x3 6.84 us: from_col(): lax.ppermute(x, 'col', [(i, (i + by) % cols) for i in range(cols)])]
    pallas_call x0 -> x2, Pallas kernels: none -> 8.98 us  [the longest x1 7.37 us: shards(): pl.pallas_call(functools.partial(product_kernel, tiles, pairs, masks, per...]
    all_gather x2 -> x0, other arithmetic: 7.09 us -> none  [shards(): lax.all_gather(select(left_vals, group), 'row', axis=0, tiled=True)]
    unnamed x1 -> x0, blocking collectives: 4.57 us -> none
  transfers between devices with their start and end apart: 3 -> 18, of which waited for: 0 -> 5; matrix products, arithmetic and copies ran while one was open for 31% -> 0% of each run, Pallas kernels for 0% -> 0%
where the time goes in v1:
time: 42.2 us; the launch traced here: 41.8 us
  starting transfers between devices  19.7 us (47%)
  waiting for transfers between devices  9.22 us (22%)
  Pallas kernels  8.98 us (21%)
  local copies, waits for them, and re-layouts  2.49 us (6%)
  between operations  0.69 us (2%)
  other arithmetic  0.67 us (2%)
    ppermute x15, starting transfers between devices, swapped(): return lax.ppermute(x, 'row', [(i, i ^ mask) for i in range(peers)])  17.3 us
    pallas_call x1, Pallas kernels, shards(): pl.pallas_call(functools.partial(product_kernel, tiles, pairs, masks, per...  7.37 us
    ppermute x3, waiting for transfers between devices, from_col(): lax.ppermute(x, 'col', [(i, (i + by) % cols) for i in range(cols)])  6.84 us
    unnamed x6, local copies, waits for them, and re-layouts  2.49 us
    ppermute x3, starting transfers between devices, from_col(): lax.ppermute(x, 'col', [(i, (i + by) % cols) for i in range(cols)])  2.46 us
    ppermute x15, waiting for transfers between devices, swapped(): return lax.ppermute(x, 'row', [(i, i ^ mask) for i in range(peers)])  2.38 us
    pallas_call x1, Pallas kernels, pack(): pl.pallas_call(pack_kernel, out_shape=jax.ShapeDtypeStruct((rows, LANES),...  1.61 us
  transfers between devices with their start and end apart: 18, of which 5 were waited for; matrix products, arithmetic and copies ran while one was open for 0% of the time, Pallas kernels for 0%

profile of v1, /device:TPU:1, one launch (start us, length us, event | category | flops | bytes accessed | tf_op | source)
XLA Modules:
  0.0 41.8 jit_solution(14188516444207983077)
XLA Ops:
  0.0 0.6 %pad_add_fusion.1.where_ref = s32[2]{0:T(128)} fusion(s32[1]{0:T(128)} %constant.9.clone.1, s32[1]{0:T(128)} %bitcast), kind=kLoop, calls=%fused_computation.1 | loop fusion | flops 2 | bytes 16 | tf_op jit(solution)/shard_map/stack | solution.py:60
  0.6 1.6 %shard_map.64.refs_7_ = bf16[272,128]{1,0:T(8,128)(2,1)} custom-call(s32[2]{0:T(128)} %pad_add_fusion.1.where_ref, s32[2,4]{1,0:T(2,128)} %bitcast.12, s32[2,8]{1,0:T(2,128)} %bitcast.13, bf16[2,4,4096]{2,1,0:T(4,128)(2,1)} %bitcast.11), custom_call_target="tpu_custom_call" | custom-call | tf_op jit(solution)/shard_map/pallas_call | solution.py:62
  2.2 4.2 %collective-permute-start.14 = (bf16[272,128]{1,0:T(8,128)(2,1)}, bf16[272,128]{1,0:T(8,128)(2,1)S(1)}, u32[]{:S(2)}, u32[]{:S(2)}) collective-permute-start(bf16[272,128]{1,0:T(8,128)(2,1)} %shard_map.64.refs_7_), channel_id=1, source_target_pairs={{0,24},{2,26},{4,28},{6,30},{8,16},{10,18},{12,20},{14,22},{16,8},... | collective-permute-start | bytes 208904 | tf_op jit(solution)/shard_map/ppermute | solution.py:19
  6.4 0.0 collective-permute-start.10
  6.4 0.3 collective-permute-start.6
  6.6 1.2 %collective-permute-start.2 = (bf16[32,4096]{1,0:T(8,128)(2,1)}, bf16[32,4096]{1,0:T(8,128)(2,1)S(1)}, u32[]{:S(2)}, u32[]{:S(2)}) collective-permute-start(bf16[32,4096]{1,0:T(8,128)(2,1)} %bitcast.7), channel_id=1, source_target_pairs={{0,1},{1,0},{2,3},{3,2},{4,5},{5,4},{6,7},{7,6},{8,9},{9,8},{10,11... | collective-permute-start | bytes 786440 | tf_op jit(solution)/shard_map/ppermute | solution.py:193
  7.9 0.3 collective-permute-start.1
  8.1 5.3 %collective-permute-done.1.refs_4_ = s32[1,1]{1,0:T(1,128)} collective-permute-done((s32[1,1]{1,0:T(1,128)}, s32[1,1]{1,0:T(1,128)}, u32[]{:S(2)}, u32[]{:S(2)}) %collective-permute-start.1) | collective-permute-done | bytes 36 | tf_op jit(solution)/shard_map/ppermute | solution.py:193
  13.4 1.0 %collective-permute-start = (s32[1,32]{1,0:T(1,128)}, s32[1,32]{1,0:T(1,128)S(1)}, u32[]{:S(2)}, u32[]{:S(2)}) collective-permute-start(s32[1,32]{1,0:T(1,128)} %bitcast.9), channel_id=1, source_target_pairs={{0,1},{1,0},{2,3},{3,2},{4,5},{5,4},{6,7},{7,6},{8,9},{9,8},{10,11... | collective-permute-start | bytes 392 | tf_op jit(solution)/shard_map/ppermute | solution.py:193
  14.4 1.5 %collective-permute-done.refs_2_ = s32[1,32]{1,0:T(1,128)S(1)} collective-permute-done((s32[1,32]{1,0:T(1,128)}, s32[1,32]{1,0:T(1,128)S(1)}, u32[]{:S(2)}, u32[]{:S(2)}) %collective-permute-start) | collective-permute-done | bytes 160 | tf_op jit(solution)/shard_map/ppermute | solution.py:193
  15.9 1.0 %collective-permute-start.4 = (bf16[272,128]{1,0:T(8,128)(2,1)}, bf16[272,128]{1,0:T(8,128)(2,1)S(1)}, u32[]{:S(2)}, u32[]{:S(2)}) collective-permute-start(bf16[272,128]{1,0:T(8,128)(2,1)} %shard_map.64.refs_7_), channel_id=1, source_target_pairs={{0,4},{2,6},{4,0},{6,2},{8,12},{10,14},{12,8},{14,10},{16,20},{18,... | collective-permute-start | bytes 208904 | tf_op jit(solution)/shard_map/ppermute | solution.py:19
  17.0 0.0 collective-permute-done.14.refs_19_
  17.0 4.0 %collective-permute-start.3 = (bf16[272,128]{1,0:T(8,128)(2,1)}, bf16[272,128]{1,0:T(8,128)(2,1)S(1)}, u32[]{:S(2)}, u32[]{:S(2)}) collective-permute-start(bf16[272,128]{1,0:T(8,128)(2,1)} %shard_map.64.refs_7_), channel_id=1, source_target_pairs={{0,2},{2,0},{4,6},{6,4},{8,10},{10,8},{12,14},{14,12},{16,18},{18,... | collective-permute-start | bytes 208904 | tf_op jit(solution)/shard_map/ppermute | solution.py:19
  20.9 0.0 collective-permute-done.10.refs_15_
  21.0 0.2 collective-permute-start.16
  21.2 0.0 collective-permute-done.6.refs_11_
  21.2 0.3 collective-permute-start.15
  21.5 0.0 collective-permute-done.4.refs_9_
  21.5 1.2 %collective-permute-start.12 = (bf16[272,128]{1,0:T(8,128)(2,1)S(1)}, bf16[272,128]{1,0:T(8,128)(2,1)S(1)}, u32[]{:S(2)}, u32[]{:S(2)}) collective-permute-start(bf16[272,128]{1,0:T(8,128)(2,1)S(1)} %collective-permute-done.10.refs_15_), channel_id=1, source_target_pairs={{0,4},{2,6},{4,0},{6,2},{8,12},{10,14},{12,8},{14,10},{16,20},{18,... | collective-permute-start | bytes 208904 | tf_op jit(solution)/shard_map/ppermute | solution.py:19
  22.8 0.0 collective-permute-done.3.refs_8_
  22.8 3.3 %collective-permute-start.11 = (bf16[272,128]{1,0:T(8,128)(2,1)S(1)}, bf16[272,128]{1,0:T(8,128)(2,1)S(1)}, u32[]{:S(2)}, u32[]{:S(2)}) collective-permute-start(bf16[272,128]{1,0:T(8,128)(2,1)S(1)} %collective-permute-done.10.refs_15_), channel_id=1, source_target_pairs={{0,2},{2,0},{4,6},{6,4},{8,10},{10,8},{12,14},{14,12},{16,18},{18,... | collective-permute-start | bytes 208904 | tf_op jit(solution)/shard_map/ppermute | solution.py:19
  26.1 0.0 collective-permute-done.16.refs_21_
  26.1 0.0 collective-permute-start.8
  26.1 0.0 collective-permute-done.15.refs_20_
  26.1 1.3 %collective-permute-start.7 = (bf16[272,128]{1,0:T(8,128)(2,1)S(1)}, bf16[272,128]{1,0:T(8,128)(2,1)S(1)}, u32[]{:S(2)}, u32[]{:S(2)}) collective-permute-start(bf16[272,128]{1,0:T(8,128)(2,1)S(1)} %collective-permute-done.6.refs_11_), channel_id=1, source_target_pairs={{0,2},{2,0},{4,6},{6,4},{8,10},{10,8},{12,14},{14,12},{16,18},{18,... | collective-permute-start | bytes 208904 | tf_op jit(solution)/shard_map/ppermute | solution.py:19
  28.0 0.0 collective-permute-done.12.refs_17_
  28.0 0.4 collective-permute-start.5
  28.5 0.0 collective-permute-done.11.refs_16_
  28.5 0.2 collective-permute-start.17
  28.6 1.2 %collective-permute-done.8.refs_13_ = bf16[272,128]{1,0:T(8,128)(2,1)S(1)} collective-permute-done((bf16[272,128]{1,0:T(8,128)(2,1)S(1)}, bf16[272,128]{1,0:T(8,128)(2,1)S(1)}, u32[]{:S(2)}, u32[]{:S(2)}) %collective-permute-start.8) | collective-permute-done | bytes 69664 | tf_op jit(solution)/shard_map/ppermute | solution.py:19
  29.8 0.9 %collective-permute-start.13 = (bf16[272,128]{1,0:T(8,128)(2,1)S(1)}, bf16[272,128]{1,0:T(8,128)(2,1)S(1)}, u32[]{:S(2)}, u32[]{:S(2)}) collective-permute-start(bf16[272,128]{1,0:T(8,128)(2,1)S(1)} %collective-permute-done.12.refs_17_), channel_id=1, source_target_pairs={{0,2},{2,0},{4,6},{6,4},{8,10},{10,8},{12,14},{14,12},{16,18},{18,... | collective-permute-start | bytes 208904 | tf_op jit(solution)/shard_map/ppermute | solution.py:19
  30.7 0.0 collective-permute-done.7.refs_12_
  30.7 0.0 collective-permute-start.9
  30.7 0.1 pad_add_fusion.refs_0_
  30.7 0.0 collective-permute-done.5.refs_10_
  30.7 0.0 collective-permute-done.17.refs_22_
  30.8 0.8 %collective-permute-done.13.refs_18_ = bf16[272,128]{1,0:T(8,128)(2,1)S(1)} collective-permute-done((bf16[272,128]{1,0:T(8,128)(2,1)S(1)}, bf16[272,128]{1,0:T(8,128)(2,1)S(1)}, u32[]{:S(2)}, u32[]{:S(2)}) %collective-permute-start.13) | collective-permute-done | bytes 69664 | tf_op jit(solution)/shard_map/ppermute | solution.py:19
  31.6 0.4 collective-permute-done.9.refs_14_
  31.9 0.0 collective-permute-done.2.refs_6_
  31.9 0.0 copy-start
  31.9 0.9 %copy-done = bf16[272,128]{1,0:T(8,128)(2,1)S(1)} copy-done((bf16[272,128]{1,0:T(8,128)(2,1)S(1)}, bf16[272,128]{1,0:T(8,128)(2,1)}, u32[]{:S(2)}) %copy-start) | copy-done | bytes 69656
  32.8 0.0 copy-start.1
  32.8 0.9 %copy-done.1 = bf16[1,1,32,4096]{3,2,1,0:T(8,128)(2,1)S(1)} copy-done((bf16[1,1,32,4096]{3,2,1,0:T(8,128)(2,1)S(1)}, bf16[1,1,32,4096]{3,2,1,0:T(8,128)(2,1)}, u32[]{:S(2)}) %copy-start.1) | copy-done | bytes 262168
  33.8 0.0 copy-start.2
  33.8 0.7 %copy-done.2 = s32[1,1,32]{2,1,0:T(1,128)S(1)} copy-done((s32[1,1,32]{2,1,0:T(1,128)S(1)}, s32[1,1,32]{2,1,0:T(1,128)}, u32[]{:S(2)}) %copy-start.2) | copy-done | bytes 152
  34.4 7.4 %shard_map.65 = f32[512,1024]{1,0:T(8,128)} custom-call(s32[2]{0:T(128)S(1)} %pad_add_fusion.refs_0_, s32[1,32]{1,0:T(1,128)S(1)} %bitcast.10, s32[1,32]{1,0:T(1,128)S(1)} %collective-permute-done.refs_2_, s32[1,1]{1,0:T(1,128)S(6)} %copy.7.refs_3_, s32[1,1]{1,0:T(1,128)} %collective-permute-done.1.refs_4_, bf16[32,4096]{1,0:T(8,128)(2,1)S(1)} %bitcast.8, ...), custom_call_target="tpu_custom_call" | custom-call | tf_op jit(solution)/shard_map/pallas_call | solution.py:212
Async XLA Ops:
  2.2 14.8 %collective-permute-start.14 = (bf16[272,128]{1,0:T(8,128)(2,1)}, bf16[272,128]{1,0:T(8,128)(2,1)S(1)}, u32[]{:S(2)}, u32[]{:S(2)}) collective-permute-start(bf16[272,128]{1,0:T(8,128)(2,1)} %shard_map.64.refs_7_), channel_id=1, source_target_pairs={{0,24},{2,26},{4,28},{6,30},{8,16},{10,18},{12,20},{14,22},{16,8},... | collective-permute-start | bytes 208904 | tf_op jit(solution)/shard_map/ppermute | solution.py:19
  6.4 14.6 %collective-permute-start.10 = (bf16[272,128]{1,0:T(8,128)(2,1)}, bf16[272,128]{1,0:T(8,128)(2,1)S(1)}, u32[]{:S(2)}, u32[]{:S(2)}) collective-permute-start(bf16[272,128]{1,0:T(8,128)(2,1)} %shard_map.64.refs_7_), channel_id=1, source_target_pairs={{0,16},{2,18},{4,20},{6,22},{8,24},{10,26},{12,28},{14,30},{16,0},... | collective-permute-start | bytes 208904 | tf_op jit(solution)/shard_map/ppermute | solution.py:19
  6.4 14.8 %collective-permute-start.6 = (bf16[272,128]{1,0:T(8,128)(2,1)}, bf16[272,128]{1,0:T(8,128)(2,1)S(1)}, u32[]{:S(2)}, u32[]{:S(2)}) collective-permute-start(bf16[272,128]{1,0:T(8,128)(2,1)} %shard_map.64.refs_7_), channel_id=1, source_target_pairs={{0,8},{2,10},{4,12},{6,14},{8,0},{10,2},{12,4},{14,6},{16,24},{18,... | collective-permute-start | bytes 208904 | tf_op jit(solution)/shard_map/ppermute | solution.py:19
  6.6 25.3 %collective-permute-start.2 = (bf16[32,4096]{1,0:T(8,128)(2,1)}, bf16[32,4096]{1,0:T(8,128)(2,1)S(1)}, u32[]{:S(2)}, u32[]{:S(2)}) collective-permute-start(bf16[32,4096]{1,0:T(8,128)(2,1)} %bitcast.7), channel_id=1, source_target_pairs={{0,1},{1,0},{2,3},{3,2},{4,5},{5,4},{6,7},{7,6},{8,9},{9,8},{10,11... | collective-permute-start | bytes 786440 | tf_op jit(solution)/shard_map/ppermute | solution.py:193
  7.9 5.6 %collective-permute-start.1 = (s32[1,1]{1,0:T(1,128)}, s32[1,1]{1,0:T(1,128)}, u32[]{:S(2)}, u32[]{:S(2)}) collective-permute-start(s32[1,1]{1,0:T(1,128)} %param.11), channel_id=1, source_target_pairs={{0,1},{1,0},{2,3},{3,2},{4,5},{5,4},{6,7},{7,6},{8,9},{9,8},{10,11... | collective-permute-start | bytes 20 | tf_op jit(solution)/shard_map/ppermute | solution.py:193
  13.4 2.5 %collective-permute-start = (s32[1,32]{1,0:T(1,128)}, s32[1,32]{1,0:T(1,128)S(1)}, u32[]{:S(2)}, u32[]{:S(2)}) collective-permute-start(s32[1,32]{1,0:T(1,128)} %bitcast.9), channel_id=1, source_target_pairs={{0,1},{1,0},{2,3},{3,2},{4,5},{5,4},{6,7},{7,6},{8,9},{9,8},{10,11... | collective-permute-start | bytes 392 | tf_op jit(solution)/shard_map/ppermute | solution.py:193
  15.9 5.6 %collective-permute-start.4 = (bf16[272,128]{1,0:T(8,128)(2,1)}, bf16[272,128]{1,0:T(8,128)(2,1)S(1)}, u32[]{:S(2)}, u32[]{:S(2)}) collective-permute-start(bf16[272,128]{1,0:T(8,128)(2,1)} %shard_map.64.refs_7_), channel_id=1, source_target_pairs={{0,4},{2,6},{4,0},{6,2},{8,12},{10,14},{12,8},{14,10},{16,20},{18,... | collective-permute-start | bytes 208904 | tf_op jit(solution)/shard_map/ppermute | solution.py:19
  17.0 5.8 %collective-permute-start.3 = (bf16[272,128]{1,0:T(8,128)(2,1)}, bf16[272,128]{1,0:T(8,128)(2,1)S(1)}, u32[]{:S(2)}, u32[]{:S(2)}) collective-permute-start(bf16[272,128]{1,0:T(8,128)(2,1)} %shard_map.64.refs_7_), channel_id=1, source_target_pairs={{0,2},{2,0},{4,6},{6,4},{8,10},{10,8},{12,14},{14,12},{16,18},{18,... | collective-permute-start | bytes 208904 | tf_op jit(solution)/shard_map/ppermute | solution.py:19
  21.0 5.1 %collective-permute-start.16 = (bf16[272,128]{1,0:T(8,128)(2,1)S(1)}, bf16[272,128]{1,0:T(8,128)(2,1)S(1)}, u32[]{:S(2)}, u32[]{:S(2)}) collective-permute-start(bf16[272,128]{1,0:T(8,128)(2,1)S(1)} %collective-permute-done.14.refs_19_), channel_id=1, source_target_pairs={{0,4},{2,6},{4,0},{6,2},{8,12},{10,14},{12,8},{14,10},{16,20},{18,... | collective-permute-start | bytes 208904 | tf_op jit(solution)/shard_map/ppermute | solution.py:19
  21.2 4.9 %collective-permute-start.15 = (bf16[272,128]{1,0:T(8,128)(2,1)S(1)}, bf16[272,128]{1,0:T(8,128)(2,1)S(1)}, u32[]{:S(2)}, u32[]{:S(2)}) collective-permute-start(bf16[272,128]{1,0:T(8,128)(2,1)S(1)} %collective-permute-done.14.refs_19_), channel_id=1, source_target_pairs={{0,2},{2,0},{4,6},{6,4},{8,10},{10,8},{12,14},{14,12},{16,18},{18,... | collective-permute-start | bytes 208904 | tf_op jit(solution)/shard_map/ppermute | solution.py:19
  21.5 6.5 %collective-permute-start.12 = (bf16[272,128]{1,0:T(8,128)(2,1)S(1)}, bf16[272,128]{1,0:T(8,128)(2,1)S(1)}, u32[]{:S(2)}, u32[]{:S(2)}) collective-permute-start(bf16[272,128]{1,0:T(8,128)(2,1)S(1)} %collective-permute-done.10.refs_15_), channel_id=1, source_target_pairs={{0,4},{2,6},{4,0},{6,2},{8,12},{10,14},{12,8},{14,10},{16,20},{18,... | collective-permute-start | bytes 208904 | tf_op jit(solution)/shard_map/ppermute | solution.py:19
  22.8 5.7 %collective-permute-start.11 = (bf16[272,128]{1,0:T(8,128)(2,1)S(1)}, bf16[272,128]{1,0:T(8,128)(2,1)S(1)}, u32[]{:S(2)}, u32[]{:S(2)}) collective-permute-start(bf16[272,128]{1,0:T(8,128)(2,1)S(1)} %collective-permute-done.10.refs_15_), channel_id=1, source_target_pairs={{0,2},{2,0},{4,6},{6,4},{8,10},{10,8},{12,14},{14,12},{16,18},{18,... | collective-permute-start | bytes 208904 | tf_op jit(solution)/shard_map/ppermute | solution.py:19
  26.1 3.7 %collective-permute-start.8 = (bf16[272,128]{1,0:T(8,128)(2,1)S(1)}, bf16[272,128]{1,0:T(8,128)(2,1)S(1)}, u32[]{:S(2)}, u32[]{:S(2)}) collective-permute-start(bf16[272,128]{1,0:T(8,128)(2,1)S(1)} %collective-permute-done.6.refs_11_), channel_id=1, source_target_pairs={{0,4},{2,6},{4,0},{6,2},{8,12},{10,14},{12,8},{14,10},{16,20},{18,... | collective-permute-start | bytes 208904 | tf_op jit(solution)/shard_map/ppermute | solution.py:19
  26.1 4.6 %collective-permute-start.7 = (bf16[272,128]{1,0:T(8,128)(2,1)S(1)}, bf16[272,128]{1,0:T(8,128)(2,1)S(1)}, u32[]{:S(2)}, u32[]{:S(2)}) collective-permute-start(bf16[272,128]{1,0:T(8,128)(2,1)S(1)} %collective-permute-done.6.refs_11_), channel_id=1, source_target_pairs={{0,2},{2,0},{4,6},{6,4},{8,10},{10,8},{12,14},{14,12},{16,18},{18,... | collective-permute-start | bytes 208904 | tf_op jit(solution)/shard_map/ppermute | solution.py:19
  28.0 2.7 %collective-permute-start.5 = (bf16[272,128]{1,0:T(8,128)(2,1)S(1)}, bf16[272,128]{1,0:T(8,128)(2,1)S(1)}, u32[]{:S(2)}, u32[]{:S(2)}) collective-permute-start(bf16[272,128]{1,0:T(8,128)(2,1)S(1)} %collective-permute-done.4.refs_9_), channel_id=1, source_target_pairs={{0,2},{2,0},{4,6},{6,4},{8,10},{10,8},{12,14},{14,12},{16,18},{18,... | collective-permute-start | bytes 208904 | tf_op jit(solution)/shard_map/ppermute | solution.py:19
  28.5 2.3 %collective-permute-start.17 = (bf16[272,128]{1,0:T(8,128)(2,1)S(1)}, bf16[272,128]{1,0:T(8,128)(2,1)S(1)}, u32[]{:S(2)}, u32[]{:S(2)}) collective-permute-start(bf16[272,128]{1,0:T(8,128)(2,1)S(1)} %collective-permute-done.16.refs_21_), channel_id=1, source_target_pairs={{0,2},{2,0},{4,6},{6,4},{8,10},{10,8},{12,14},{14,12},{16,18},{18,... | collective-permute-start | bytes 208904 | tf_op jit(solution)/shard_map/ppermute | solution.py:19
  29.8 1.8 %collective-permute-start.13 = (bf16[272,128]{1,0:T(8,128)(2,1)S(1)}, bf16[272,128]{1,0:T(8,128)(2,1)S(1)}, u32[]{:S(2)}, u32[]{:S(2)}) collective-permute-start(bf16[272,128]{1,0:T(8,128)(2,1)S(1)} %collective-permute-done.12.refs_17_), channel_id=1, source_target_pairs={{0,2},{2,0},{4,6},{6,4},{8,10},{10,8},{12,14},{14,12},{16,18},{18,... | collective-permute-start | bytes 208904 | tf_op jit(solution)/shard_map/ppermute | solution.py:19
  30.7 1.3 %collective-permute-start.9 = (bf16[272,128]{1,0:T(8,128)(2,1)S(1)}, bf16[272,128]{1,0:T(8,128)(2,1)S(1)}, u32[]{:S(2)}, u32[]{:S(2)}) collective-permute-start(bf16[272,128]{1,0:T(8,128)(2,1)S(1)} %collective-permute-done.8.refs_13_), channel_id=1, source_target_pairs={{0,2},{2,0},{4,6},{6,4},{8,10},{10,8},{12,14},{14,12},{16,18},{18,... | collective-permute-start | bytes 208904 | tf_op jit(solution)/shard_map/ppermute | solution.py:19
  31.9 0.9 %copy-start = (bf16[272,128]{1,0:T(8,128)(2,1)S(1)}, bf16[272,128]{1,0:T(8,128)(2,1)}, u32[]{:S(2)}) copy-start(bf16[272,128]{1,0:T(8,128)(2,1)} %shard_map.64.refs_7_) | copy-start | bytes 208900
  32.8 0.9 %copy-start.1 = (bf16[1,1,32,4096]{3,2,1,0:T(8,128)(2,1)S(1)}, bf16[1,1,32,4096]{3,2,1,0:T(8,128)(2,1)}, u32[]{:S(2)}) copy-start(bf16[1,1,32,4096]{3,2,1,0:T(8,128)(2,1)} %param.9) | copy-start | bytes 786436
  33.8 0.7 %copy-start.2 = (s32[1,1,32]{2,1,0:T(1,128)S(1)}, s32[1,1,32]{2,1,0:T(1,128)}, u32[]{:S(2)}) copy-start(s32[1,1,32]{2,1,0:T(1,128)} %param.10) | copy-start | bytes 388

commit v2 on v1

v2 whole, which is shorter than its diff:
```python
import functools
import math

import jax
import jax.numpy as jnp
from jax import lax
from jax.experimental import pallas as pl
from jax.experimental.pallas import tpu as pltpu
from jax.sharding import PartitionSpec as P

KB = 16
BCR = 16
LANES = 128
META = 16


def swapped(x, mask):
    peers = lax.axis_size("row")
    return lax.ppermute(x, "row", [(i, i ^ mask) for i in range(peers)])


def low_half(rows):
    return lax.broadcasted_iota(jnp.int32, (rows, LANES), 1) < LANES // 2


def pick_lane(row, at):
    lane = lax.broadcasted_iota(jnp.int32, row.shape, 1)
    return jnp.sum(jnp.where(lane == at, row, 0.0), axis=1, keepdims=True)


def pack_kernel(start, masks, slots_ref, lengths_ref, left_ref, *refs):
    out_ref, tall, square = refs[-3:]
    tiles, own, _ = left_ref.shape
    peers = lax.axis_size("row")
    me = lax.axis_index("row")
    mask = masks[0] if masks[0] == masks[1] else jnp.where(lax.rem(me, 2) == 0, masks[0], masks[1])
    per_row = peers * own // lengths_ref.shape[1]
    first = lax.bitwise_xor(me, mask) * own
    row = lax.div(first, per_row)
    place = lax.rem(first, per_row)
    group = lax.axis_index("col")
    low = low_half(32)
    low_meta = low_half(META)
    meta_row = lax.broadcasted_iota(jnp.int32, (META, LANES), 0)
    meta = jnp.full((META, LANES), -1.0, jnp.float32)
    at = 0
    for by in range(tiles):
        m = lax.rem(group - by + tiles, tiles)
        values = left_ref[m].astype(jnp.float32)
        for t in range(32):
            tall[pl.ds(by % 2 * 256 + t * 8, own), :] = values[:, t * LANES : (t + 1) * LANES]
        named = slots_ref[pl.ds(m, 1), :].astype(jnp.float32)
        live = pick_lane(lengths_ref[pl.ds(m, 1), :].astype(jnp.float32), row)
        for s in range(0, own, 2):
            one = tall[pl.ds(by % 2 * 256 + s, 32, stride=8), :]
            two = tall[pl.ds(by % 2 * 256 + s + 1, 32, stride=8), :]
            even = jnp.where(low, one, pltpu.roll(two, LANES // 2, 1))
            odd = jnp.where(low, pltpu.roll(one, LANES // 2, 1), two)
            y = square.at[at % 4]
            y[pl.ds(0, 32, stride=2), :] = even
            y[pl.ds(1, 32, stride=2), :] = odd
            out_ref[start + at * 64 : start + at * 64 + 64, :] = y[...].astype(out_ref.dtype)
            a = jnp.where((place + s).astype(jnp.float32) < live, pick_lane(named, s), -1.0)
            b = jnp.where((place + s + 1).astype(jnp.float32) < live, pick_lane(named, s + 1), -1.0)
            meta = jnp.where(meta_row == at, jnp.where(low_meta, a, b), meta)
            at += 1
    out_ref[start + at * 64 : start + at * 64 + META, :] = meta.astype(out_ref.dtype)


def pack(left, slots, lengths, masks=(0, 0), parts=1, part=0, buffer=None):
    tiles, own, _ = left.shape
    rows = tiles * own // 2 * 64 + META
    vmem = pl.BlockSpec(memory_space=pltpu.VMEM)
    given = [] if buffer is None else [buffer]
    return pl.pallas_call(
        functools.partial(pack_kernel, part * rows, masks),
        out_shape=jax.ShapeDtypeStruct((parts * rows, LANES), left.dtype),
        in_specs=[vmem] * (3 + len(given)),
        out_specs=vmem,
        scratch_shapes=[pltpu.VMEM((512, LANES), jnp.float32), pltpu.VMEM((4, 64, LANES), jnp.float32)],
        input_output_aliases={3: 0} if given else {},
        compiler_params=pltpu.CompilerParams(vmem_limit_bytes=4 * 1024 * 1024),
        cost_estimate=pl.CostEstimate(flops=1000000, bytes_accessed=1000, transcendentals=0),
    )(slots, lengths, left, *given)


def spots_kernel(count_ref, places_ref, out_ref):
    slot = lax.broadcasted_iota(jnp.int32, places_ref.shape, 1)
    out_ref[...] = jnp.where(slot < count_ref[0, 0], places_ref[...], -1)


def live_spots(places, count):
    smem, vmem = pl.BlockSpec(memory_space=pltpu.SMEM), pl.BlockSpec(memory_space=pltpu.VMEM)
    return pl.pallas_call(
        spots_kernel,
        out_shape=jax.ShapeDtypeStruct(places.shape, places.dtype),
        in_specs=[smem, vmem],
        out_specs=vmem,
        compiler_params=pltpu.CompilerParams(vmem_limit_bytes=1024 * 1024),
    )(count, places)


def repeat(count, body):
    if count <= 2:
        for i in range(count):
            body(i)
    else:
        pl.loop(0, count)(body)


def right_kernel(places_ref, values_ref, dense_ref, tall, square):
    slots = values_ref.shape[0]
    half = lax.broadcasted_iota(jnp.int32, (32, LANES), 1) // (LANES // 2)
    dense_ref[...] = jnp.zeros_like(dense_ref)

    def some(g):
        values = values_ref[pl.ds(g * 16, 16), :].astype(jnp.float32)
        for t in range(32):
            tall[pl.ds(t * 16, 16), :] = values[:, t * LANES : (t + 1) * LANES]
        for s in range(16):
            spot = places_ref[0, g * 16 + s]
            live = spot >= 0
            spot = jnp.maximum(spot, 0)
            k, j = lax.shift_right_logical(spot, 4), lax.bitwise_and(spot, 15)
            side = lax.bitwise_and(j, 1)
            plain = tall[pl.ds(s, 32, stride=16), :]
            turned = pltpu.roll(plain, LANES // 2, 1)
            keep = half == jnp.where(live, side, -1)
            even = jnp.where(keep, jnp.where(side == 0, plain, turned), 0.0)
            odd = jnp.where(keep, jnp.where(side == 0, turned, plain), 0.0)
            y = square.at[s % square.shape[0]]
            y[pl.ds(0, 32, stride=2), :] = even
            y[pl.ds(1, 32, stride=2), :] = odd
            at = (
                pl.ds(pl.multiple_of(k * 64, 64), 64),
                pl.ds(pl.multiple_of(lax.shift_right_logical(j, 1) * LANES, LANES), LANES),
            )
            dense_ref[at] = dense_ref[at] + y[...].astype(dense_ref.dtype)

    repeat(slots // 16, some)


def dense_right(values, spots):
    side = math.isqrt(values.shape[1])
    smem, vmem = pl.BlockSpec(memory_space=pltpu.SMEM), pl.BlockSpec(memory_space=pltpu.VMEM)
    return pl.pallas_call(
        right_kernel,
        out_shape=jax.ShapeDtypeStruct((KB * side, BCR * side), values.dtype),
        in_specs=[smem, vmem],
        out_specs=vmem,
        scratch_shapes=[pltpu.VMEM((512, LANES), jnp.float32), pltpu.VMEM((4, side, LANES), jnp.float32)],
        compiler_params=pltpu.CompilerParams(vmem_limit_bytes=16 * 1024 * 1024),
        cost_estimate=pl.CostEstimate(flops=1300000000, bytes_accessed=1000, transcendentals=0),
    )(spots, values)


def place_left(parcels, row, tiles, pairs, dense_ref, names_ref):
    half = (lax.broadcasted_iota(jnp.int32, (16, LANES), 1) // (LANES // 2)).astype(jnp.float32)
    body = tiles * pairs * 64
    for i, (parcel, start) in enumerate(parcels):
        names_ref[i * META : i * META + META, :] = parcel[pl.ds(start + body, META), :].astype(jnp.float32)

    def one(m):
        names = []
        for i, (parcel, start) in enumerate(parcels):
            for p in range(pairs):
                at = m * pairs + p
                name = jnp.broadcast_to(names_ref[pl.ds(i * META + at, 1), :], (16, LANES))
                turned = pltpu.roll(name, LANES // 2, 1)
                names.append((parcel, start + at * 64, (name - half).astype(jnp.bfloat16), (turned - half).astype(jnp.bfloat16)))
        plain, turned = [], []
        for parcel, start, _, _ in names:
            v = [parcel[pl.ds(start + c * 16, 16), :] for c in range(4)]
            plain.append(v)
            turned.append([pltpu.roll(x.astype(jnp.float32), LANES // 2, 1).astype(x.dtype) for x in v])
        for t in range(KB // 2):
            want = jnp.bfloat16(2 * t)
            hits = [(a == want, b == want) for _, _, a, b in names]
            for c in range(4):
                acc = jnp.zeros((16, LANES), dense_ref.dtype)
                for (a, b), v, w in zip(hits, plain, turned):
                    acc = jnp.where(a, v[c], acc)
                    acc = jnp.where(b, w[c], acc)
                dense_ref[
                    pl.ds(row * 64 + c * 16, 16),
                    pl.ds(pl.multiple_of(m * KB * 64 + t * LANES, LANES), LANES),
                ] = acc

    repeat(tiles, one)


def product_kernel(tiles, pairs, jobs, stacks, first_call, *refs):
    rights, refs = refs[:tiles], refs[tiles:]
    held, refs = refs[:stacks], refs[stacks:]
    if not first_call:
        refs = refs[1:]
    out_ref, left_dense, result, names, sems = refs
    sharing = names.shape[0] // META
    size = tiles * pairs * 64 + META
    me = lax.axis_index("row")
    core = lax.rem(me, 2)

    def pick(pair):
        return pair[0] if pair[0] == pair[1] else jnp.where(core == 0, pair[0], pair[1])

    for i, (_, parts) in enumerate(jobs):
        parcels = []
        for at, zero, one in parts:
            start = pick((zero * size, one * size))
            parcels.append((held[at], start if isinstance(start, int) else pl.multiple_of(start, 16)))
        place_left(parcels, i, tiles, pairs, left_dense, names)
    width = 256
    depth = rights[0].shape[0]
    copies = []
    for n in range(out_ref.shape[1] // width):
        span = slice(n * width, n * width + width)
        total = None
        for m in range(tiles):
            part = jnp.dot(
                left_dense[:, m * depth : m * depth + depth],
                rights[m][:, span],
                preferred_element_type=jnp.float32,
            )
            total = part if total is None else total + part
        result[:, span] = total
        if n % 2 == 1:
            wide = slice(n * width - width, n * width + width)
            for i, (masks, _) in enumerate(jobs):
                row = lax.div(lax.bitwise_xor(me, pick(masks)), sharing)
                copies.append(
                    pltpu.make_async_copy(
                        result.at[pl.ds(i * 64, 64), wide],
                        out_ref.at[pl.ds(pl.multiple_of(row * 64, 64), 64), wide],
                        sems.at[n // 2, i],
                    )
                )
                copies[-1].start()
    for copy in copies:
        copy.wait()


def product(rights, stacks, jobs, sharing, height, pairs, before=None):
    depth, width = rights[0].shape
    tiles, dtype = len(rights), rights[0].dtype
    rows = len(jobs) * 64
    vmem, hbm = pl.BlockSpec(memory_space=pltpu.VMEM), pl.BlockSpec(memory_space=pltpu.HBM)
    first = before is None
    return pl.pallas_call(
        functools.partial(product_kernel, tiles, pairs, jobs, len(stacks), first),
        out_shape=jax.ShapeDtypeStruct((height, width), jnp.float32),
        in_specs=[vmem] * (tiles + len(stacks)) + ([] if first else [hbm]),
        out_specs=hbm,
        scratch_shapes=[
            pltpu.VMEM((rows, tiles * depth), dtype),
            pltpu.VMEM((rows, width), jnp.float32),
            pltpu.VMEM((sharing * META, LANES), jnp.float32),
            pltpu.SemaphoreType.DMA((width // 512, len(jobs))),
        ],
        input_output_aliases={} if first else {tiles + len(stacks): 0},
        compiler_params=pltpu.CompilerParams(vmem_limit_bytes=(8 + 5 * tiles) * 1024 * 1024),
        cost_estimate=pl.CostEstimate(
            flops=2000000000, bytes_accessed=1000, transcendentals=0
        ),
    )(*rights, *stacks, *([] if first else [before]))


def fill_kernel(start, part_ref, *refs):
    refs[-1][start : start + part_ref.shape[0], :] = part_ref[...]


def fill(part, rows, start=0, buffer=None):
    vmem = pl.BlockSpec(memory_space=pltpu.VMEM)
    given = [] if buffer is None else [buffer]
    return pl.pallas_call(
        functools.partial(fill_kernel, start),
        out_shape=jax.ShapeDtypeStruct((rows, LANES), part.dtype),
        in_specs=[vmem] * (1 + len(given)),
        out_specs=vmem,
        input_output_aliases={1: 0} if given else {},
        compiler_params=pltpu.CompilerParams(vmem_limit_bytes=4 * 1024 * 1024),
        cost_estimate=pl.CostEstimate(flops=1000000, bytes_accessed=1000, transcendentals=0),
    )(part, *given)


def by_core(x, zero, one):
    peers = lax.axis_size("row")
    return lax.ppermute(x, "row", [(i, i ^ (one if i % 2 else zero)) for i in range(peers)])


def spread(order):
    names = [0]
    for mask in order:
        names = names + [name ^ mask for name in names]
    return names


def shards(left_blocks, left_slots, left_lengths, right_blocks, right_places, right_count):
    peers = lax.axis_size("row")
    cols = lax.axis_size("col")
    tiles, own = left_blocks.shape[1], left_blocks.shape[2]
    block_rows = left_lengths.shape[2]
    sharing = peers // block_rows
    side = math.isqrt(left_blocks.shape[-1])
    height = block_rows * side

    def from_col(x, by):
        return x if by == 0 else lax.ppermute(x, "col", [(i, (i + by) % cols) for i in range(cols)])

    left, slots, lengths = left_blocks[0], left_slots[0], left_lengths[0]
    own_right = right_blocks[0, 0]

    if sharing == 2:
        bits = [1 << b for b in range(1, peers.bit_length() - 1)]
        zero = bits[-1:] + bits[:-1]
        one = bits[-1:] + bits[1:-1] + bits[:1]
        first = (zero[0], one[0])
        come = by_core(left, *first), by_core(slots, *first)
        stack = pack(left, slots, lengths, parts=2)
        sending, stack = lax.optimization_barrier((own_right, stack))
        stack = pack(come[0], come[1], lengths, first, parts=2, part=1, buffer=stack)
        rights = []
        for step, (a, b) in enumerate(zip(zero[1:-1], one[1:-1])):
            new = by_core(stack, a, b)
            rows = stack.shape[0]
            wide = fill(stack, 2 * rows)
            if step == 0:
                wide, places, count = lax.optimization_barrier((wide, right_places[0], right_count))
                spots = live_spots(places, count)
                sent = [from_col(sending, by) for by in range(1, cols)]
                places = [from_col(spots, by) for by in range(1, cols)]
            stack = fill(new, 2 * rows, rows, wide)
        late, stack = lax.optimization_barrier((spots, stack))
        rights = [dense_right(own_right, late)]
        rights += [dense_right(x, p) for x, p in zip(sent, places)]
        last = by_core(stack, zero[-1], one[-1])
        held = [[stack, last], [swapped(stack, 1), None]]
        at_zero, at_one = spread(zero), spread(one)
        count = len(at_zero) // 2
        kinds = {}
        for name in at_zero:
            p, q = at_zero.index(name), at_one.index(name)
            kinds.setdefault((p // count, q // count), []).append((name, p % count, q % count))

        def jobs(mine, theirs):
            zeros, ones = kinds.get((mine, theirs), []), kinds.get((theirs, mine), [])
            return [
                ((a, b), (mine, a_own, b_own), (theirs, a_other, b_other))
                for (a, a_own, a_other), (b, b_other, b_own) in zip(zeros, ones)
            ]

        out = None
        for group in ([(0, 0)], [(1, 0)], [(0, 1), (1, 1)]):
            arrays, keys, listed = [], {}, []

            def key(whose, part):
                if (whose, part) not in keys:
                    keys[whose, part] = len(arrays)
                    arrays.append(held[whose][part])
                return keys[whose, part]

            for mine, theirs in group:
                for masks, (m, x, y), (t, u, v) in jobs(mine, theirs):
                    listed.append((masks, [(key(0, m), x, y), (key(1, t), u, v)]))
            if listed:
                out = product(rights, arrays, listed, sharing, height, own // 2, out)
            if held[1][1] is None:
                held[0][1], out = lax.optimization_barrier((held[0][1], out))
                held[1][1] = swapped(held[0][1], 1)
        return out
    spots = live_spots(right_places[0], right_count)
    rights = [dense_right(from_col(own_right, by), from_col(spots, by)) for by in range(cols)]
    parcel = pack(left, slots, lengths)
    held = {0: parcel}
    for mask in range(4, peers, 4):
        held[mask] = swapped(parcel, mask)
    for mask in range(0, peers, 4):
        held[mask + 2] = swapped(held[mask], 2)
    for mask in range(0, peers, 2):
        held[mask + 1] = swapped(held[mask], 1)
    half = None
    for names in (range(peers // 2), range(peers // 2, peers)):
        listed = [
            ((names[i], names[i]), [(i + j, 0, 0) for j in range(sharing)]) for i in range(0, len(names), sharing)
        ]
        half = product(rights, [held[n] for n in names], listed, sharing, height, own // 2, half)
    return half


def solution(mesh):
    return jax.shard_map(
        shards,
        mesh=mesh,
        in_specs=(
            P("col", None, "row", None),
            P("col", None, "row"),
            P("col", None, None),
            P("col", "row", None, None),
            P("col", "row", None),
            P("col", "row"),
        ),
        out_specs=P("col", "row"),
        check_vma=False,
    )
```

time: 42.2 us -> 27.3 us (0.65)
  starting transfers between devices: 19.7 us -> 10.5 us
  waiting for transfers between devices: 9.22 us -> 2.96 us
  local copies, waits for them, and re-layouts: 2.49 us -> 3.8 us
  other arithmetic: 0.67 us -> 0 us
    ppermute x15 -> x2, starting transfers between devices: 17.3 us -> 3.21 us  [swapped(): return lax.ppermute(x, 'row', [(i, i ^ mask) for i in range(peers)])]
    ppermute x3 -> x2, waiting for transfers between devices: 6.84 us -> 0.01 us  [from_col(): lax.ppermute(x, 'col', [(i, (i + by) % cols) for i in range(cols)])]
    ppermute x0 -> x4, starting transfers between devices: none -> 4.88 us  [by_core(): lax.ppermute(x, 'row', [(i, i ^ (one if i % 2 else zero)) for i in range(...]
    ppermute x0 -> x4, waiting for transfers between devices: none -> 2.95 us  [by_core(): lax.ppermute(x, 'row', [(i, i ^ (one if i % 2 else zero)) for i in range(...]
    ppermute x15 -> x2, waiting for transfers between devices: 2.38 us -> 0.01 us  [swapped(): return lax.ppermute(x, 'row', [(i, i ^ mask) for i in range(peers)])]
    unnamed x6 -> x10, local copies, waits for them, and re-layouts: 2.49 us -> 3.8 us
    another operation x2 -> x0, other arithmetic: 0.67 us -> none  [the longest x1 0.6 us: pack(): jnp.stack([lax.axis_index('row').astype(jnp.int32), jnp.int32(per_row)])]
    pallas_call x2 -> x10, Pallas kernels: 8.98 us -> 9.03 us  [the longest x3 6.27 us: product(): pl.pallas_call(functools.partial(product_kernel, tiles, pairs, jobs, len(...]
  transfers between devices with their start and end apart: 18 -> 8, of which waited for: 5 -> 2; matrix products, arithmetic and copies ran while one was open for 0% -> 0% of each run, Pallas kernels for 0% -> 23%
where the time goes in v2:
time: 27.3 us; the launch traced here: 27.1 us
  starting transfers between devices  10.5 us (38%)
  Pallas kernels  9.03 us (33%)
  local copies, waits for them, and re-layouts  3.8 us (14%)
  waiting for transfers between devices  2.96 us (11%)
  between operations  0.76 us (3%)
    pallas_call x3, Pallas kernels, product(): pl.pallas_call(functools.partial(product_kernel, tiles, pairs, jobs, len(...  6.27 us
    ppermute x4, starting transfers between devices, by_core(): lax.ppermute(x, 'row', [(i, i ^ (one if i % 2 else zero)) for i in range(...  4.88 us
    unnamed x10, local copies, waits for them, and re-layouts  3.8 us
    ppermute x2, starting transfers between devices, swapped(): return lax.ppermute(x, 'row', [(i, i ^ mask) for i in range(peers)])  3.21 us
    ppermute x4, waiting for transfers between devices, by_core(): lax.ppermute(x, 'row', [(i, i ^ (one if i % 2 else zero)) for i in range(...  2.95 us
    ppermute x2, starting transfers between devices, from_col(): lax.ppermute(x, 'col', [(i, (i + by) % cols) for i in range(cols)])  2.44 us
    pallas_call x2, Pallas kernels, dense_right(): pl.pallas_call(right_kernel, out_shape=jax.ShapeDtypeStruct((KB * side, B...  2.35 us
  transfers between devices with their start and end apart: 8, of which 2 were waited for; matrix products, arithmetic and copies ran while one was open for 0% of the time, Pallas kernels for 23%

profile of v2, /device:TPU:1, one launch (start us, length us, event | category | flops | bytes accessed | tf_op | source)
XLA Modules:
  0.0 27.1 jit_solution(7716340369660493959)
XLA Ops:
  0.0 3.1 %collective-permute-start.1 = (bf16[2,4,4096]{2,1,0:T(4,128)(2,1)}, bf16[2,4,4096]{2,1,0:T(4,128)(2,1)S(1)}, u32[]{:S(2)}, u32[]{:S(2)}) collective-permute-start(bf16[2,4,4096]{2,1,0:T(4,128)(2,1)} %bitcast.5), channel_id=1, source_target_pairs={{0,16},{2,18},{4,20},{6,22},{8,24},{10,26},{12,28},{14,30},{16,0},... | collective-permute-start | bytes 196616 | tf_op jit(solution)/shard_map/ppermute | solution.py:287
  3.1 0.0 collective-permute-start
  3.2 0.0 copy-start
  3.2 0.8 %copy-done = bf16[1,2,4,4096]{3,2,1,0:T(4,128)(2,1)S(1)} copy-done((bf16[1,2,4,4096]{3,2,1,0:T(4,128)(2,1)S(1)}, bf16[1,2,4,4096]{3,2,1,0:T(4,128)(2,1)}, u32[]{:S(2)}) %copy-start) | copy-done | bytes 65560
  4.0 0.0 copy-start.1
  4.0 0.7 %copy-done.1 = s32[1,2,8]{2,1,0:T(2,128)S(1)} copy-done((s32[1,2,8]{2,1,0:T(2,128)S(1)}, s32[1,2,8]{2,1,0:T(2,128)}, u32[]{:S(2)}) %copy-start.1) | copy-done | bytes 88
  4.7 0.0 copy-start.2
  4.7 0.7 %copy-done.2 = s32[1,2,4]{2,1,0:T(2,128)S(1)} copy-done((s32[1,2,4]{2,1,0:T(2,128)S(1)}, s32[1,2,4]{2,1,0:T(2,128)}, u32[]{:S(2)}) %copy-start.2) | copy-done | bytes 56
  5.4 0.2 shard_map.64.refs_0_
  5.6 2.0 %collective-permute-done.slots_ref = s32[2,4]{1,0:T(2,128)S(1)} collective-permute-done((s32[2,4]{1,0:T(2,128)}, s32[2,4]{1,0:T(2,128)S(1)}, u32[]{:S(2)}, u32[]{:S(2)}) %collective-permute-start) | collective-permute-done | bytes 64 | tf_op jit(solution)/shard_map/ppermute | solution.py:287
  7.6 0.0 collective-permute-done.1.left_ref
  7.6 0.2 shard_map.65.part_ref
  7.8 0.5 %collective-permute-start.2 = (bf16[544,128]{1,0:T(8,128)(2,1)S(1)}, bf16[544,128]{1,0:T(8,128)(2,1)S(1)}, u32[]{:S(2)}, u32[]{:S(2)}) collective-permute-start(bf16[544,128]{1,0:T(8,128)(2,1)S(1)} %shard_map.65.part_ref), channel_id=1, source_target_pairs={{0,4},{2,10},{4,0},{6,14},{8,12},{10,2},{12,8},{14,6},{16,20},{18,... | collective-permute-start | bytes 417800 | tf_op jit(solution)/shard_map/ppermute | solution.py:287
  8.2 1.2 %collective-permute-start.4 = (bf16[32,4096]{1,0:T(8,128)(2,1)}, bf16[32,4096]{1,0:T(8,128)(2,1)S(1)}, u32[]{:S(2)}, u32[]{:S(2)}) collective-permute-start(bf16[32,4096]{1,0:T(8,128)(2,1)} %bitcast.11), channel_id=1, source_target_pairs={{0,1},{1,0},{2,3},{3,2},{4,5},{5,4},{6,7},{7,6},{8,9},{9,8},{10,11... | collective-permute-start | bytes 786440 | tf_op jit(solution)/shard_map/ppermute | solution.py:307
  10.1 0.0 copy-start.4
  10.1 0.6 %copy-done.4 = s32[1,1,32]{2,1,0:T(1,128)S(1)} copy-done((s32[1,1,32]{2,1,0:T(1,128)S(1)}, s32[1,1,32]{2,1,0:T(1,128)}, u32[]{:S(2)}) %copy-start.4) | copy-done | bytes 152
  10.8 1.0 %collective-permute-done.2.part_ref = bf16[544,128]{1,0:T(8,128)(2,1)S(1)} collective-permute-done((bf16[544,128]{1,0:T(8,128)(2,1)S(1)}, bf16[544,128]{1,0:T(8,128)(2,1)S(1)}, u32[]{:S(2)}, u32[]{:S(2)}) %collective-permute-start.2) | collective-permute-done | bytes 139296 | tf_op jit(solution)/shard_map/ppermute | solution.py:287
  11.7 2.4 %collective-permute-start.6 = (bf16[1088,128]{1,0:T(8,128)(2,1)S(1)}, bf16[1088,128]{1,0:T(8,128)(2,1)S(1)}, u32[]{:S(2)}, u32[]{:S(2)}) collective-permute-start(bf16[1088,128]{1,0:T(8,128)(2,1)S(1)} %shard_map.68.refs_2_), channel_id=1, source_target_pairs={{0,2},{2,0},{4,6},{6,4},{8,10},{10,8},{12,14},{14,12},{16,18},{18,... | collective-permute-start | bytes 835592 | tf_op jit(solution)/shard_map/ppermute | solution.py:19
  14.2 1.2 %collective-permute-start.3 = (s32[1,32]{1,0:T(1,128)S(1)}, s32[1,32]{1,0:T(1,128)S(1)}, u32[]{:S(2)}, u32[]{:S(2)}) collective-permute-start(s32[1,32]{1,0:T(1,128)S(1)} %shard_map.67.places_ref), channel_id=1, source_target_pairs={{0,1},{1,0},{2,3},{3,2},{4,5},{5,4},{6,7},{7,6},{8,9},{9,8},{10,11... | collective-permute-start | bytes 392 | tf_op jit(solution)/shard_map/ppermute | solution.py:307
  15.4 1.2 %collective-permute-start.5 = (bf16[1088,128]{1,0:T(8,128)(2,1)S(1)}, bf16[1088,128]{1,0:T(8,128)(2,1)S(1)}, u32[]{:S(2)}, u32[]{:S(2)}) collective-permute-start(bf16[1088,128]{1,0:T(8,128)(2,1)S(1)} %shard_map.68.refs_2_), channel_id=1, source_target_pairs={{0,8},{2,6},{4,12},{6,2},{8,0},{10,14},{12,4},{14,10},{16,24},{18,... | collective-permute-start | bytes 835592 | tf_op jit(solution)/shard_map/ppermute | solution.py:287
  16.6 0.0 copy-start.3
  16.6 0.9 %copy-done.3 = bf16[1,1,32,4096]{3,2,1,0:T(8,128)(2,1)S(1)} copy-done((bf16[1,1,32,4096]{3,2,1,0:T(8,128)(2,1)S(1)}, bf16[1,1,32,4096]{3,2,1,0:T(8,128)(2,1)}, u32[]{:S(2)}) %copy-start.3) | copy-done | bytes 262168
  17.6 1.2 %shard_map.69.refs_0_ = bf16[1024,1024]{1,0:T(8,128)(2,1)S(1)} custom-call(s32[1,32]{1,0:T(1,128)S(1)} %shard_map.67.places_ref, bf16[32,4096]{1,0:T(8,128)(2,1)S(1)} %bitcast.12), custom_call_target="tpu_custom_call" | custom-call | flops 1300000000 | bytes 1000 | tf_op jit(solution)/shard_map/pallas_call | solution.py:146
  18.8 0.0 collective-permute-done.3.places_ref
  18.8 0.0 collective-permute-done.4.values_ref
  18.8 1.2 %shard_map.70.refs_1_ = bf16[1024,1024]{1,0:T(8,128)(2,1)S(1)} custom-call(s32[1,32]{1,0:T(1,128)S(1)} %collective-permute-done.3.places_ref, bf16[32,4096]{1,0:T(8,128)(2,1)S(1)} %collective-permute-done.4.values_ref), custom_call_target="tpu_custom_call" | custom-call | flops 1300000000 | bytes 1000 | tf_op jit(solution)/shard_map/pallas_call | solution.py:146
  20.0 0.0 collective-permute-done.6.refs_3_
  20.0 1.8 %shard_map.71.refs_4_ = f32[512,1024]{1,0:T(8,128)} custom-call(bf16[1024,1024]{1,0:T(8,128)(2,1)S(1)} %shard_map.69.refs_0_, bf16[1024,1024]{1,0:T(8,128)(2,1)S(1)} %shard_map.70.refs_1_, bf16[1088,128]{1,0:T(8,128)(2,1)S(1)} %shard_map.68.refs_2_, bf16[1088,128]{1,0:T(8,128)(2,1)S(1)} %collective-permute-done.6.refs_3_), custom_call_target="tpu_custom_call" | custom-call | flops 2000000000 | bytes 1000 | tf_op jit(solution)/shard_map/pallas_call | solution.py:248
  21.8 0.0 collective-permute-done.5.refs_2_.refs_4_
  21.8 0.8 %collective-permute-start.7 = (bf16[1088,128]{1,0:T(8,128)(2,1)S(1)}, bf16[1088,128]{1,0:T(8,128)(2,1)S(1)}, u32[]{:S(2)}, u32[]{:S(2)}) collective-permute-start(bf16[1088,128]{1,0:T(8,128)(2,1)S(1)} %collective-permute-done.5.refs_2_.refs_4_), channel_id=1, source_target_pairs={{0,2},{2,0},{4,6},{6,4},{8,10},{10,8},{12,14},{14,12},{16,18},{18,... | collective-permute-start | bytes 835592 | tf_op jit(solution)/shard_map/ppermute | solution.py:19
  22.6 1.8 %shard_map.72.refs_5_ = f32[512,1024]{1,0:T(8,128)} custom-call(bf16[1024,1024]{1,0:T(8,128)(2,1)S(1)} %shard_map.69.refs_0_, bf16[1024,1024]{1,0:T(8,128)(2,1)S(1)} %shard_map.70.refs_1_, bf16[1088,128]{1,0:T(8,128)(2,1)S(1)} %collective-permute-done.5.refs_2_.refs_4_, ...), custom_call_target="tpu_custom_call", output_to_operand_aliasing={{}: (4, {})} | custom-call | flops 2000000000 | bytes 1000 | tf_op jit(solution)/shard_map/pallas_call | solution.py:248
  24.4 0.0 collective-permute-done.7.refs_3_
  24.4 2.7 %shard_map.73 = f32[512,1024]{1,0:T(8,128)} custom-call(bf16[1024,1024]{1,0:T(8,128)(2,1)S(1)} %shard_map.69.refs_0_, bf16[1024,1024]{1,0:T(8,128)(2,1)S(1)} %shard_map.70.refs_1_, bf16[1088,128]{1,0:T(8,128)(2,1)S(1)} %shard_map.68.refs_2_, bf16[1088,128]{1,0:T(8,128)(2,1)S(1)} %collective-permute-done.7.refs_3_, ...), custom_call_target="tpu_custom_call", output_to_operand_aliasing={{}: (5, {})} | custom-call | flops 2000000000 | bytes 1000 | tf_op jit(solution)/shard_map/pallas_call | solution.py:248
  (3 shorter events, 0.0 us)
Async XLA Ops:
  0.0 7.6 %collective-permute-start.1 = (bf16[2,4,4096]{2,1,0:T(4,128)(2,1)}, bf16[2,4,4096]{2,1,0:T(4,128)(2,1)S(1)}, u32[]{:S(2)}, u32[]{:S(2)}) collective-permute-start(bf16[2,4,4096]{2,1,0:T(4,128)(2,1)} %bitcast.5), channel_id=1, source_target_pairs={{0,16},{2,18},{4,20},{6,22},{8,24},{10,26},{12,28},{14,30},{16,0},... | collective-permute-start | bytes 196616 | tf_op jit(solution)/shard_map/ppermute | solution.py:287
  3.1 4.4 %collective-permute-start = (s32[2,4]{1,0:T(2,128)}, s32[2,4]{1,0:T(2,128)S(1)}, u32[]{:S(2)}, u32[]{:S(2)}) collective-permute-start(s32[2,4]{1,0:T(2,128)} %bitcast.9), channel_id=1, source_target_pairs={{0,16},{2,18},{4,20},{6,22},{8,24},{10,26},{12,28},{14,30},{16,0},... | collective-permute-start | bytes 104 | tf_op jit(solution)/shard_map/ppermute | solution.py:287
  3.2 0.8 %copy-start = (bf16[1,2,4,4096]{3,2,1,0:T(4,128)(2,1)S(1)}, bf16[1,2,4,4096]{3,2,1,0:T(4,128)(2,1)}, u32[]{:S(2)}) copy-start(bf16[1,2,4,4096]{3,2,1,0:T(4,128)(2,1)} %param.6) | copy-start | bytes 196612
  4.0 0.7 %copy-start.1 = (s32[1,2,8]{2,1,0:T(2,128)S(1)}, s32[1,2,8]{2,1,0:T(2,128)}, u32[]{:S(2)}) copy-start(s32[1,2,8]{2,1,0:T(2,128)} %param.8) | copy-start | bytes 196
  4.7 0.7 %copy-start.2 = (s32[1,2,4]{2,1,0:T(2,128)S(1)}, s32[1,2,4]{2,1,0:T(2,128)}, u32[]{:S(2)}) copy-start(s32[1,2,4]{2,1,0:T(2,128)} %param.7) | copy-start | bytes 100
  7.8 4.0 %collective-permute-start.2 = (bf16[544,128]{1,0:T(8,128)(2,1)S(1)}, bf16[544,128]{1,0:T(8,128)(2,1)S(1)}, u32[]{:S(2)}, u32[]{:S(2)}) collective-permute-start(bf16[544,128]{1,0:T(8,128)(2,1)S(1)} %shard_map.65.part_ref), channel_id=1, source_target_pairs={{0,4},{2,10},{4,0},{6,14},{8,12},{10,2},{12,8},{14,6},{16,20},{18,... | collective-permute-start | bytes 417800 | tf_op jit(solution)/shard_map/ppermute | solution.py:287
  8.2 10.6 %collective-permute-start.4 = (bf16[32,4096]{1,0:T(8,128)(2,1)}, bf16[32,4096]{1,0:T(8,128)(2,1)S(1)}, u32[]{:S(2)}, u32[]{:S(2)}) collective-permute-start(bf16[32,4096]{1,0:T(8,128)(2,1)} %bitcast.11), channel_id=1, source_target_pairs={{0,1},{1,0},{2,3},{3,2},{4,5},{5,4},{6,7},{7,6},{8,9},{9,8},{10,11... | collective-permute-start | bytes 786440 | tf_op jit(solution)/shard_map/ppermute | solution.py:307
  10.1 0.7 %copy-start.4 = (s32[1,1,32]{2,1,0:T(1,128)S(1)}, s32[1,1,32]{2,1,0:T(1,128)}, u32[]{:S(2)}) copy-start(s32[1,1,32]{2,1,0:T(1,128)} %param.10) | copy-start | bytes 388
  11.7 8.2 %collective-permute-start.6 = (bf16[1088,128]{1,0:T(8,128)(2,1)S(1)}, bf16[1088,128]{1,0:T(8,128)(2,1)S(1)}, u32[]{:S(2)}, u32[]{:S(2)}) collective-permute-start(bf16[1088,128]{1,0:T(8,128)(2,1)S(1)} %shard_map.68.refs_2_), channel_id=1, source_target_pairs={{0,2},{2,0},{4,6},{6,4},{8,10},{10,8},{12,14},{14,12},{16,18},{18,... | collective-permute-start | bytes 835592 | tf_op jit(solution)/shard_map/ppermute | solution.py:19
  14.2 4.6 %collective-permute-start.3 = (s32[1,32]{1,0:T(1,128)S(1)}, s32[1,32]{1,0:T(1,128)S(1)}, u32[]{:S(2)}, u32[]{:S(2)}) collective-permute-start(s32[1,32]{1,0:T(1,128)S(1)} %shard_map.67.places_ref), channel_id=1, source_target_pairs={{0,1},{1,0},{2,3},{3,2},{4,5},{5,4},{6,7},{7,6},{8,9},{9,8},{10,11... | collective-permute-start | bytes 392 | tf_op jit(solution)/shard_map/ppermute | solution.py:307
  15.4 6.4 %collective-permute-start.5 = (bf16[1088,128]{1,0:T(8,128)(2,1)S(1)}, bf16[1088,128]{1,0:T(8,128)(2,1)S(1)}, u32[]{:S(2)}, u32[]{:S(2)}) collective-permute-start(bf16[1088,128]{1,0:T(8,128)(2,1)S(1)} %shard_map.68.refs_2_), channel_id=1, source_target_pairs={{0,8},{2,6},{4,12},{6,2},{8,0},{10,14},{12,4},{14,10},{16,24},{18,... | collective-permute-start | bytes 835592 | tf_op jit(solution)/shard_map/ppermute | solution.py:287
  16.6 0.9 %copy-start.3 = (bf16[1,1,32,4096]{3,2,1,0:T(8,128)(2,1)S(1)}, bf16[1,1,32,4096]{3,2,1,0:T(8,128)(2,1)}, u32[]{:S(2)}) copy-start(bf16[1,1,32,4096]{3,2,1,0:T(8,128)(2,1)} %param.9) | copy-start | bytes 786436
  21.8 2.6 %collective-permute-start.7 = (bf16[1088,128]{1,0:T(8,128)(2,1)S(1)}, bf16[1088,128]{1,0:T(8,128)(2,1)S(1)}, u32[]{:S(2)}, u32[]{:S(2)}) collective-permute-start(bf16[1088,128]{1,0:T(8,128)(2,1)S(1)} %collective-permute-done.5.refs_2_.refs_4_), channel_id=1, source_target_pairs={{0,2},{2,0},{4,6},{6,4},{8,10},{10,8},{12,14},{14,12},{16,18},{18,... | collective-permute-start | bytes 835592 | tf_op jit(solution)/shard_map/ppermute | solution.py:19

commit v3 on v2

--- a/solution.py
+++ b/solution.py
@@ -80,7 +80,7 @@
         scratch_shapes=[pltpu.VMEM((512, LANES), jnp.float32), pltpu.VMEM((4, 64, LANES), jnp.float32)],
         input_output_aliases={3: 0} if given else {},
         compiler_params=pltpu.CompilerParams(vmem_limit_bytes=4 * 1024 * 1024),
-        cost_estimate=pl.CostEstimate(flops=1000000, bytes_accessed=1000, transcendentals=0),
+        cost_estimate=pl.CostEstimate(flops=2 * 10**9, bytes_accessed=1000, transcendentals=0),
     )(slots, lengths, left, *given)
 
 
@@ -97,6 +97,7 @@
         in_specs=[smem, vmem],
         out_specs=vmem,
         compiler_params=pltpu.CompilerParams(vmem_limit_bytes=1024 * 1024),
+        cost_estimate=pl.CostEstimate(flops=10**9, bytes_accessed=1000, transcendentals=0),
     )(count, places)
 
 
@@ -140,7 +141,7 @@
     repeat(slots // 16, some)
 
 
-def dense_right(values, spots):
+def dense_right(values, spots, work=0):
     side = math.isqrt(values.shape[1])
     smem, vmem = pl.BlockSpec(memory_space=pltpu.SMEM), pl.BlockSpec(memory_space=pltpu.VMEM)
     return pl.pallas_call(
@@ -150,7 +151,7 @@
         out_specs=vmem,
         scratch_shapes=[pltpu.VMEM((512, LANES), jnp.float32), pltpu.VMEM((4, side, LANES), jnp.float32)],
         compiler_params=pltpu.CompilerParams(vmem_limit_bytes=16 * 1024 * 1024),
-        cost_estimate=pl.CostEstimate(flops=1300000000, bytes_accessed=1000, transcendentals=0),
+        cost_estimate=pl.CostEstimate(flops=work, bytes_accessed=1000, transcendentals=0),
     )(spots, values)
 
 
@@ -259,7 +260,7 @@
         input_output_aliases={} if first else {tiles + len(stacks): 0},
         compiler_params=pltpu.CompilerParams(vmem_limit_bytes=(8 + 5 * tiles) * 1024 * 1024),
         cost_estimate=pl.CostEstimate(
-            flops=2000000000, bytes_accessed=1000, transcendentals=0
+            flops=10**6, bytes_accessed=1000, transcendentals=0
         ),
     )(*rights, *stacks, *([] if first else [before]))
 
@@ -317,8 +318,9 @@
         come = by_core(left, *first), by_core(slots, *first)
         stack = pack(left, slots, lengths, parts=2)
         sending, stack = lax.optimization_barrier((own_right, stack))
+        sent = [from_col(sending, by) for by in range(1, cols)]
         stack = pack(come[0], come[1], lengths, first, parts=2, part=1, buffer=stack)
-        rights = []
+        held = [[stack], [swapped(stack, 1)]]
         for step, (a, b) in enumerate(zip(zero[1:-1], one[1:-1])):
             new = by_core(stack, a, b)
             rows = stack.shape[0]
@@ -326,20 +328,28 @@
             if step == 0:
                 wide, places, count = lax.optimization_barrier((wide, right_places[0], right_count))
                 spots = live_spots(places, count)
-                sent = [from_col(sending, by) for by in range(1, cols)]
                 places = [from_col(spots, by) for by in range(1, cols)]
+                rights = [dense_right(own_right, spots, 13 * 10**8)]
+                new, rights[0], sent, places = lax.optimization_barrier((new, rights[0], sent, places))
+            held[0].append(new)
+            held[1].append(swapped(new, 1))
             stack = fill(new, 2 * rows, rows, wide)
-        late, stack = lax.optimization_barrier((spots, stack))
-        rights = [dense_right(own_right, late)]
         rights += [dense_right(x, p) for x, p in zip(sent, places)]
-        last = by_core(stack, zero[-1], one[-1])
-        held = [[stack, last], [swapped(stack, 1), None]]
-        at_zero, at_one = spread(zero), spread(one)
-        count = len(at_zero) // 2
+        held[0].append(by_core(stack, zero[-1], one[-1]))
+        final = len(held[0]) - 1
+
+        def spread_at(order):
+            found = {}
+            for p, name in enumerate(spread(order)):
+                part = max(p.bit_length() - 1, 0)
+                found[name] = (part, p - (1 << part if part else 0))
+            return found
+
+        at_zero, at_one = spread_at(zero), spread_at(one)
         kinds = {}
-        for name in at_zero:
-            p, q = at_zero.index(name), at_one.index(name)
-            kinds.setdefault((p // count, q // count), []).append((name, p % count, q % count))
+        for name, (p, x) in at_zero.items():
+            q, y = at_one[name]
+            kinds.setdefault((p, q), []).append((name, x, y))
 
         def jobs(mine, theirs):
             zeros, ones = kinds.get((mine, theirs), []), kinds.get((theirs, mine), [])
@@ -348,8 +358,14 @@
                 for (a, a_own, a_other), (b, b_other, b_own) in zip(zeros, ones)
             ]
 
+        early = range(final)
+        groups = [
+            [(p, q) for p in early for q in early],
+            [(final, q) for q in early],
+            [(p, final) for p in range(final + 1)],
+        ]
         out = None
-        for group in ([(0, 0)], [(1, 0)], [(0, 1), (1, 1)]):
+        for group in groups:
             arrays, keys, listed = [], {}, []
 
             def key(whose, part):
@@ -363,9 +379,9 @@
                     listed.append((masks, [(key(0, m), x, y), (key(1, t), u, v)]))
             if listed:
                 out = product(rights, arrays, listed, sharing, height, own // 2, out)
-            if held[1][1] is None:
-                held[0][1], out = lax.optimization_barrier((held[0][1], out))
-                held[1][1] = swapped(held[0][1], 1)
+            if len(held[1]) == final:
+                held[0][final], held[1], out = lax.optimization_barrier((held[0][final], held[1], out))
+                held[1].append(swapped(held[0][final], 1))
         return out
     spots = live_spots(right_places[0], right_count)
     rights = [dense_right(from_col(own_right, by), from_col(spots, by)) for by in range(cols)]

time: 27.3 us -> 26.6 us (0.974)
  starting transfers between devices: 10.5 us -> 11.7 us
  waiting for transfers between devices: 2.96 us -> 1.77 us
  local copies, waits for them, and re-layouts: 3.8 us -> 2.99 us
    ppermute x4, waiting for transfers between devices: 2.95 us -> 0.01 us  [by_core(): lax.ppermute(x, 'row', [(i, i ^ (one if i % 2 else zero)) for i in range(...]
    ppermute x2, waiting for transfers between devices: 0.01 us -> 1.75 us  [from_col(): lax.ppermute(x, 'col', [(i, (i + by) % cols) for i in range(cols)])]
    ppermute x2 -> x3, starting transfers between devices: 3.21 us -> 4.54 us  [swapped(): return lax.ppermute(x, 'row', [(i, i ^ mask) for i in range(peers)])]
    ppermute x2, starting transfers between devices: 2.44 us -> 1.62 us  [from_col(): lax.ppermute(x, 'col', [(i, (i + by) % cols) for i in range(cols)])]
    unnamed x10, local copies, waits for them, and re-layouts: 3.8 us -> 2.99 us
    ppermute x4, starting transfers between devices: 4.88 us -> 5.56 us  [by_core(): lax.ppermute(x, 'row', [(i, i ^ (one if i % 2 else zero)) for i in range(...]
  transfers between devices with their start and end apart: 8 -> 9, of which waited for: 2 -> 1; matrix products, arithmetic and copies ran while one was open for 0% -> 0% of each run, Pallas kernels for 23% -> 24%
where the time goes in v3:
time: 26.6 us; the launch traced here: 26.4 us
  starting transfers between devices  11.7 us (44%)
  Pallas kernels  9.11 us (34%)
  local copies, waits for them, and re-layouts  2.99 us (11%)
  waiting for transfers between devices  1.77 us (7%)
  between operations  0.78 us (3%)
    pallas_call x3, Pallas kernels, product(): pl.pallas_call(functools.partial(product_kernel, tiles, pairs, jobs, len(...  6.3 us
    ppermute x4, starting transfers between devices, by_core(): lax.ppermute(x, 'row', [(i, i ^ (one if i % 2 else zero)) for i in range(...  5.56 us
    ppermute x3, starting transfers between devices, swapped(): return lax.ppermute(x, 'row', [(i, i ^ mask) for i in range(peers)])  4.54 us
    unnamed x10, local copies, waits for them, and re-layouts  2.99 us
    pallas_call x2, Pallas kernels, dense_right(): pl.pallas_call(right_kernel, out_shape=jax.ShapeDtypeStruct((KB * side, B...  2.39 us
    ppermute x2, waiting for transfers between devices, from_col(): lax.ppermute(x, 'col', [(i, (i + by) % cols) for i in range(cols)])  1.75 us
    ppermute x2, starting transfers between devices, from_col(): lax.ppermute(x, 'col', [(i, (i + by) % cols) for i in range(cols)])  1.62 us
  transfers between devices with their start and end apart: 9, of which 1 were waited for; matrix products, arithmetic and copies ran while one was open for 0% of the time, Pallas kernels for 24%

profile of v3, /device:TPU:1, one launch (start us, length us, event | category | flops | bytes accessed | tf_op | source)
XLA Modules:
  0.0 26.4 jit_solution(2181521591624481584)
XLA Ops:
  0.0 3.1 %collective-permute-start = (s32[2,4]{1,0:T(2,128)}, s32[2,4]{1,0:T(2,128)S(1)}, u32[]{:S(2)}, u32[]{:S(2)}) collective-permute-start(s32[2,4]{1,0:T(2,128)} %bitcast.9), channel_id=1, source_target_pairs={{0,16},{2,18},{4,20},{6,22},{8,24},{10,26},{12,28},{14,30},{16,0},... | collective-permute-start | bytes 104 | tf_op jit(solution)/shard_map/ppermute | solution.py:288
  3.1 0.0 collective-permute-start.1
  3.2 0.0 copy-start.1
  3.2 0.9 %copy-done.1 = bf16[1,2,4,4096]{3,2,1,0:T(4,128)(2,1)S(1)} copy-done((bf16[1,2,4,4096]{3,2,1,0:T(4,128)(2,1)S(1)}, bf16[1,2,4,4096]{3,2,1,0:T(4,128)(2,1)}, u32[]{:S(2)}) %copy-start.1) | copy-done | bytes 65560
  4.0 0.0 copy-start.2
  4.0 0.7 %copy-done.2 = s32[1,2,4]{2,1,0:T(2,128)S(1)} copy-done((s32[1,2,4]{2,1,0:T(2,128)S(1)}, s32[1,2,4]{2,1,0:T(2,128)}, u32[]{:S(2)}) %copy-start.2) | copy-done | bytes 56
  4.7 0.0 copy-start.3
  4.7 0.7 %copy-done.3 = s32[1,2,8]{2,1,0:T(2,128)S(1)} copy-done((s32[1,2,8]{2,1,0:T(2,128)S(1)}, s32[1,2,8]{2,1,0:T(2,128)}, u32[]{:S(2)}) %copy-start.3) | copy-done | bytes 88
  5.4 0.0 copy-start
  5.4 0.2 shard_map.64.refs_0_
  5.6 0.8 %copy-done = bf16[1,1,32,4096]{3,2,1,0:T(8,128)(2,1)S(1)} copy-done((bf16[1,1,32,4096]{3,2,1,0:T(8,128)(2,1)S(1)}, bf16[1,1,32,4096]{3,2,1,0:T(8,128)(2,1)}, u32[]{:S(2)}) %copy-start) | copy-done | bytes 262168
  6.4 1.2 %collective-permute-start.3 = (bf16[32,4096]{1,0:T(8,128)(2,1)S(1)}, bf16[32,4096]{1,0:T(8,128)(2,1)S(1)}, u32[]{:S(2)}, u32[]{:S(2)}) collective-permute-start(bf16[32,4096]{1,0:T(8,128)(2,1)S(1)} %bitcast.5), channel_id=1, source_target_pairs={{0,1},{1,0},{2,3},{3,2},{4,5},{5,4},{6,7},{7,6},{8,9},{9,8},{10,11... | collective-permute-start | bytes 786440 | tf_op jit(solution)/shard_map/ppermute | solution.py:308
  8.2 0.0 copy-start.4
  8.3 0.0 collective-permute-done.slots_ref
  8.3 0.0 collective-permute-done.1.left_ref
  8.3 0.2 shard_map.65.part_ref.refs_2_
  8.5 1.4 %collective-permute-start.2 = (bf16[544,128]{1,0:T(8,128)(2,1)S(1)}, bf16[544,128]{1,0:T(8,128)(2,1)S(1)}, u32[]{:S(2)}, u32[]{:S(2)}) collective-permute-start(bf16[544,128]{1,0:T(8,128)(2,1)S(1)} %shard_map.65.part_ref.refs_2_), channel_id=1, source_target_pairs={{0,4},{2,10},{4,0},{6,14},{8,12},{10,2},{12,8},{14,6},{16,20},{18,... | collective-permute-start | bytes 417800 | tf_op jit(solution)/shard_map/ppermute | solution.py:288
  9.9 0.0 copy-done.4
  9.9 0.4 %collective-permute-start.4 = (s32[1,32]{1,0:T(1,128)S(1)}, s32[1,32]{1,0:T(1,128)S(1)}, u32[]{:S(2)}, u32[]{:S(2)}) collective-permute-start(s32[1,32]{1,0:T(1,128)S(1)} %shard_map.67.places_ref), channel_id=1, source_target_pairs={{0,1},{1,0},{2,3},{3,2},{4,5},{5,4},{6,7},{7,6},{8,9},{9,8},{10,11... | collective-permute-start | bytes 392 | tf_op jit(solution)/shard_map/ppermute | solution.py:308
  10.3 1.2 %shard_map.68.refs_0_ = bf16[1024,1024]{1,0:T(8,128)(2,1)S(1)} custom-call(s32[1,32]{1,0:T(1,128)S(1)} %shard_map.67.places_ref, bf16[32,4096]{1,0:T(8,128)(2,1)S(1)} %bitcast.6), custom_call_target="tpu_custom_call" | custom-call | flops 1300000000 | bytes 1000 | tf_op jit(solution)/shard_map/pallas_call | solution.py:147
  11.5 1.8 %collective-permute-done.4.places_ref = s32[1,32]{1,0:T(1,128)S(1)} collective-permute-done((s32[1,32]{1,0:T(1,128)S(1)}, s32[1,32]{1,0:T(1,128)S(1)}, u32[]{:S(2)}, u32[]{:S(2)}) %collective-permute-start.4) | collective-permute-done | bytes 160 | tf_op jit(solution)/shard_map/ppermute | solution.py:308
  13.2 0.0 collective-permute-done.2.part_ref.refs_2_
  13.2 0.0 collective-permute-done.3.values_ref
  13.2 1.0 %collective-permute-start.5 = (bf16[1088,128]{1,0:T(8,128)(2,1)S(1)}, bf16[1088,128]{1,0:T(8,128)(2,1)S(1)}, u32[]{:S(2)}, u32[]{:S(2)}) collective-permute-start(bf16[1088,128]{1,0:T(8,128)(2,1)S(1)} %shard_map.70), channel_id=1, source_target_pairs={{0,8},{2,6},{4,12},{6,2},{8,0},{10,14},{12,4},{14,10},{16,24},{18,... | collective-permute-start | bytes 835592 | tf_op jit(solution)/shard_map/ppermute | solution.py:288
  14.3 2.6 %collective-permute-start.6 = (bf16[544,128]{1,0:T(8,128)(2,1)S(1)}, bf16[544,128]{1,0:T(8,128)(2,1)S(1)}, u32[]{:S(2)}, u32[]{:S(2)}) collective-permute-start(bf16[544,128]{1,0:T(8,128)(2,1)S(1)} %shard_map.65.part_ref.refs_2_), channel_id=1, source_target_pairs={{0,2},{2,0},{4,6},{6,4},{8,10},{10,8},{12,14},{14,12},{16,18},{18,... | collective-permute-start | bytes 417800 | tf_op jit(solution)/shard_map/ppermute | solution.py:19
  16.9 0.0 collective-permute-start.7
  16.9 1.2 %shard_map.69.refs_1_ = bf16[1024,1024]{1,0:T(8,128)(2,1)S(1)} custom-call(s32[1,32]{1,0:T(1,128)S(1)} %collective-permute-done.4.places_ref, bf16[32,4096]{1,0:T(8,128)(2,1)S(1)} %collective-permute-done.3.values_ref), custom_call_target="tpu_custom_call" | custom-call | bytes 1000 | tf_op jit(solution)/shard_map/pallas_call | solution.py:147
  18.1 0.0 collective-permute-done.6.refs_3_
  18.1 1.8 %shard_map.71.refs_4_ = f32[512,1024]{1,0:T(8,128)} custom-call(bf16[1024,1024]{1,0:T(8,128)(2,1)S(1)} %shard_map.68.refs_0_, bf16[1024,1024]{1,0:T(8,128)(2,1)S(1)} %shard_map.69.refs_1_, bf16[544,128]{1,0:T(8,128)(2,1)S(1)} %shard_map.65.part_ref.refs_2_, bf16[544,128]{1,0:T(8,128)(2,1)S(1)} %collective-permute-done.6.refs_3_), custom_call_target="tpu_custom_call" | custom-call | flops 1000000 | bytes 1000 | tf_op jit(solution)/shard_map/pallas_call | solution.py:249
  19.9 0.0 collective-permute-done.7.refs_3_
  19.9 0.0 collective-permute-done.5.refs_2_.refs_4_
  19.9 1.9 %collective-permute-start.8 = (bf16[1088,128]{1,0:T(8,128)(2,1)S(1)}, bf16[1088,128]{1,0:T(8,128)(2,1)S(1)}, u32[]{:S(2)}, u32[]{:S(2)}) collective-permute-start(bf16[1088,128]{1,0:T(8,128)(2,1)S(1)} %collective-permute-done.5.refs_2_.refs_4_), channel_id=1, source_target_pairs={{0,2},{2,0},{4,6},{6,4},{8,10},{10,8},{12,14},{14,12},{16,18},{18,... | collective-permute-start | bytes 835592 | tf_op jit(solution)/shard_map/ppermute | solution.py:19
  21.9 1.8 %shard_map.72.refs_5_ = f32[512,1024]{1,0:T(8,128)} custom-call(bf16[1024,1024]{1,0:T(8,128)(2,1)S(1)} %shard_map.68.refs_0_, bf16[1024,1024]{1,0:T(8,128)(2,1)S(1)} %shard_map.69.refs_1_, bf16[1088,128]{1,0:T(8,128)(2,1)S(1)} %collective-permute-done.5.refs_2_.refs_4_, ...), custom_call_target="tpu_custom_call", output_to_operand_aliasing={{}: (4, {})} | custom-call | flops 1000000 | bytes 1000 | tf_op jit(solution)/shard_map/pallas_call | solution.py:249
  23.7 0.0 collective-permute-done.8.refs_3_
  23.7 2.7 %shard_map.73 = f32[512,1024]{1,0:T(8,128)} custom-call(bf16[1024,1024]{1,0:T(8,128)(2,1)S(1)} %shard_map.68.refs_0_, bf16[1024,1024]{1,0:T(8,128)(2,1)S(1)} %shard_map.69.refs_1_, bf16[544,128]{1,0:T(8,128)(2,1)S(1)} %collective-permute-done.2.part_ref.refs_2_, ...), custom_call_target="tpu_custom_call", output_to_operand_aliasing={{}: (5, {})} | custom-call | flops 1000000 | bytes 1000 | tf_op jit(solution)/shard_map/pallas_call | solution.py:249
  (3 shorter events, 0.0 us)
Async XLA Ops:
  0.0 8.3 %collective-permute-start = (s32[2,4]{1,0:T(2,128)}, s32[2,4]{1,0:T(2,128)S(1)}, u32[]{:S(2)}, u32[]{:S(2)}) collective-permute-start(s32[2,4]{1,0:T(2,128)} %bitcast.9), channel_id=1, source_target_pairs={{0,16},{2,18},{4,20},{6,22},{8,24},{10,26},{12,28},{14,30},{16,0},... | collective-permute-start | bytes 104 | tf_op jit(solution)/shard_map/ppermute | solution.py:288
  3.1 5.1 %collective-permute-start.1 = (bf16[2,4,4096]{2,1,0:T(4,128)(2,1)}, bf16[2,4,4096]{2,1,0:T(4,128)(2,1)S(1)}, u32[]{:S(2)}, u32[]{:S(2)}) collective-permute-start(bf16[2,4,4096]{2,1,0:T(4,128)(2,1)} %bitcast.7), channel_id=1, source_target_pairs={{0,16},{2,18},{4,20},{6,22},{8,24},{10,26},{12,28},{14,30},{16,0},... | collective-permute-start | bytes 196616 | tf_op jit(solution)/shard_map/ppermute | solution.py:288
  3.2 0.9 %copy-start.1 = (bf16[1,2,4,4096]{3,2,1,0:T(4,128)(2,1)S(1)}, bf16[1,2,4,4096]{3,2,1,0:T(4,128)(2,1)}, u32[]{:S(2)}) copy-start(bf16[1,2,4,4096]{3,2,1,0:T(4,128)(2,1)} %param.6) | copy-start | bytes 196612
  4.0 0.7 %copy-start.2 = (s32[1,2,4]{2,1,0:T(2,128)S(1)}, s32[1,2,4]{2,1,0:T(2,128)}, u32[]{:S(2)}) copy-start(s32[1,2,4]{2,1,0:T(2,128)} %param.7) | copy-start | bytes 100
  4.7 0.7 %copy-start.3 = (s32[1,2,8]{2,1,0:T(2,128)S(1)}, s32[1,2,8]{2,1,0:T(2,128)}, u32[]{:S(2)}) copy-start(s32[1,2,8]{2,1,0:T(2,128)} %param.8) | copy-start | bytes 196
  5.4 0.9 %copy-start = (bf16[1,1,32,4096]{3,2,1,0:T(8,128)(2,1)S(1)}, bf16[1,1,32,4096]{3,2,1,0:T(8,128)(2,1)}, u32[]{:S(2)}) copy-start(bf16[1,1,32,4096]{3,2,1,0:T(8,128)(2,1)} %param.9) | copy-start | bytes 786436
  6.4 6.9 %collective-permute-start.3 = (bf16[32,4096]{1,0:T(8,128)(2,1)S(1)}, bf16[32,4096]{1,0:T(8,128)(2,1)S(1)}, u32[]{:S(2)}, u32[]{:S(2)}) collective-permute-start(bf16[32,4096]{1,0:T(8,128)(2,1)S(1)} %bitcast.5), channel_id=1, source_target_pairs={{0,1},{1,0},{2,3},{3,2},{4,5},{5,4},{6,7},{7,6},{8,9},{9,8},{10,11... | collective-permute-start | bytes 786440 | tf_op jit(solution)/shard_map/ppermute | solution.py:308
  8.2 1.6 %copy-start.4 = (s32[1,1,32]{2,1,0:T(1,128)S(1)}, s32[1,1,32]{2,1,0:T(1,128)}, u32[]{:S(2)}) copy-start(s32[1,1,32]{2,1,0:T(1,128)} %param.10) | copy-start | bytes 388
  8.5 4.7 %collective-permute-start.2 = (bf16[544,128]{1,0:T(8,128)(2,1)S(1)}, bf16[544,128]{1,0:T(8,128)(2,1)S(1)}, u32[]{:S(2)}, u32[]{:S(2)}) collective-permute-start(bf16[544,128]{1,0:T(8,128)(2,1)S(1)} %shard_map.65.part_ref.refs_2_), channel_id=1, source_target_pairs={{0,4},{2,10},{4,0},{6,14},{8,12},{10,2},{12,8},{14,6},{16,20},{18,... | collective-permute-start | bytes 417800 | tf_op jit(solution)/shard_map/ppermute | solution.py:288
  9.9 3.3 %collective-permute-start.4 = (s32[1,32]{1,0:T(1,128)S(1)}, s32[1,32]{1,0:T(1,128)S(1)}, u32[]{:S(2)}, u32[]{:S(2)}) collective-permute-start(s32[1,32]{1,0:T(1,128)S(1)} %shard_map.67.places_ref), channel_id=1, source_target_pairs={{0,1},{1,0},{2,3},{3,2},{4,5},{5,4},{6,7},{7,6},{8,9},{9,8},{10,11... | collective-permute-start | bytes 392 | tf_op jit(solution)/shard_map/ppermute | solution.py:308
  13.2 6.7 %collective-permute-start.5 = (bf16[1088,128]{1,0:T(8,128)(2,1)S(1)}, bf16[1088,128]{1,0:T(8,128)(2,1)S(1)}, u32[]{:S(2)}, u32[]{:S(2)}) collective-permute-start(bf16[1088,128]{1,0:T(8,128)(2,1)S(1)} %shard_map.70), channel_id=1, source_target_pairs={{0,8},{2,6},{4,12},{6,2},{8,0},{10,14},{12,4},{14,10},{16,24},{18,... | collective-permute-start | bytes 835592 | tf_op jit(solution)/shard_map/ppermute | solution.py:288
  14.3 3.8 %collective-permute-start.6 = (bf16[544,128]{1,0:T(8,128)(2,1)S(1)}, bf16[544,128]{1,0:T(8,128)(2,1)S(1)}, u32[]{:S(2)}, u32[]{:S(2)}) collective-permute-start(bf16[544,128]{1,0:T(8,128)(2,1)S(1)} %shard_map.65.part_ref.refs_2_), channel_id=1, source_target_pairs={{0,2},{2,0},{4,6},{6,4},{8,10},{10,8},{12,14},{14,12},{16,18},{18,... | collective-permute-start | bytes 417800 | tf_op jit(solution)/shard_map/ppermute | solution.py:19
  16.9 3.0 %collective-permute-start.7 = (bf16[544,128]{1,0:T(8,128)(2,1)S(1)}, bf16[544,128]{1,0:T(8,128)(2,1)S(1)}, u32[]{:S(2)}, u32[]{:S(2)}) collective-permute-start(bf16[544,128]{1,0:T(8,128)(2,1)S(1)} %collective-permute-done.2.part_ref.refs_2_), channel_id=1, source_target_pairs={{0,2},{2,0},{4,6},{6,4},{8,10},{10,8},{12,14},{14,12},{16,18},{18,... | collective-permute-start | bytes 417800 | tf_op jit(solution)/shard_map/ppermute | solution.py:19
  19.9 3.7 %collective-permute-start.8 = (bf16[1088,128]{1,0:T(8,128)(2,1)S(1)}, bf16[1088,128]{1,0:T(8,128)(2,1)S(1)}, u32[]{:S(2)}, u32[]{:S(2)}) collective-permute-start(bf16[1088,128]{1,0:T(8,128)(2,1)S(1)} %collective-permute-done.5.refs_2_.refs_4_), channel_id=1, source_target_pairs={{0,2},{2,0},{4,6},{6,4},{8,10},{10,8},{12,14},{14,12},{16,18},{18,... | collective-permute-start | bytes 835592 | tf_op jit(solution)/shard_map/ppermute | solution.py:19

commit v4 on v3

--- a/solution.py
+++ b/solution.py
@@ -80,25 +80,13 @@
         scratch_shapes=[pltpu.VMEM((512, LANES), jnp.float32), pltpu.VMEM((4, 64, LANES), jnp.float32)],
         input_output_aliases={3: 0} if given else {},
         compiler_params=pltpu.CompilerParams(vmem_limit_bytes=4 * 1024 * 1024),
-        cost_estimate=pl.CostEstimate(flops=2 * 10**9, bytes_accessed=1000, transcendentals=0),
+        cost_estimate=pl.CostEstimate(flops=3 * 10**8, bytes_accessed=1000, transcendentals=0),
     )(slots, lengths, left, *given)
 
 
-def spots_kernel(count_ref, places_ref, out_ref):
-    slot = lax.broadcasted_iota(jnp.int32, places_ref.shape, 1)
-    out_ref[...] = jnp.where(slot < count_ref[0, 0], places_ref[...], -1)
-
-
 def live_spots(places, count):
-    smem, vmem = pl.BlockSpec(memory_space=pltpu.SMEM), pl.BlockSpec(memory_space=pltpu.VMEM)
-    return pl.pallas_call(
-        spots_kernel,
-        out_shape=jax.ShapeDtypeStruct(places.shape, places.dtype),
-        in_specs=[smem, vmem],
-        out_specs=vmem,
-        compiler_params=pltpu.CompilerParams(vmem_limit_bytes=1024 * 1024),
-        cost_estimate=pl.CostEstimate(flops=10**9, bytes_accessed=1000, transcendentals=0),
-    )(count, places)
+    slot = lax.broadcasted_iota(jnp.int32, places.shape, 1)
+    return jnp.where(slot < count, places, -1)
 
 
 def repeat(count, body):

time: 26.6 us -> 26 us (0.977)
  local copies, waits for them, and re-layouts: 2.99 us -> 2.21 us
    unnamed x10, local copies, waits for them, and re-layouts: 2.99 us -> 2.21 us
  transfers between devices with their start and end apart: 9 -> 9, of which waited for: 1 -> 1; matrix products, arithmetic and copies ran while one was open for 0% -> 0% of each run, Pallas kernels for 24% -> 25%
where the time goes in v4:
time: 26 us; the launch traced here: 25.8 us
  starting transfers between devices  11.7 us (45%)
  Pallas kernels  9.1 us (35%)
  local copies, waits for them, and re-layouts  2.21 us (8%)
  waiting for transfers between devices  2.03 us (8%)
  between operations  0.76 us (3%)
    pallas_call x3, Pallas kernels, product(): pl.pallas_call(functools.partial(product_kernel, tiles, pairs, jobs, len(...  6.3 us
    ppermute x4, starting transfers between devices, by_core(): lax.ppermute(x, 'row', [(i, i ^ (one if i % 2 else zero)) for i in range(...  5.59 us
    ppermute x3, starting transfers between devices, swapped(): return lax.ppermute(x, 'row', [(i, i ^ mask) for i in range(peers)])  4.47 us
    pallas_call x2, Pallas kernels, dense_right(): pl.pallas_call(right_kernel, out_shape=jax.ShapeDtypeStruct((KB * side, B...  2.39 us
    unnamed x10, local copies, waits for them, and re-layouts  2.21 us
    ppermute x2, waiting for transfers between devices, from_col(): lax.ppermute(x, 'col', [(i, (i + by) % cols) for i in range(cols)])  1.99 us
    ppermute x2, starting transfers between devices, from_col(): lax.ppermute(x, 'col', [(i, (i + by) % cols) for i in range(cols)])  1.66 us
  transfers between devices with their start and end apart: 9, of which 1 were waited for; matrix products, arithmetic and copies ran while one was open for 0% of the time, Pallas kernels for 25%

profile of v4, /device:TPU:1, one launch (start us, length us, event | category | flops | bytes accessed | tf_op | source)
XLA Modules:
  0.0 25.8 jit_solution(14242908367638866002)
XLA Ops:
  0.0 0.0 copy-start
  0.0 3.1 %collective-permute-start.1 = (bf16[2,4,4096]{2,1,0:T(4,128)(2,1)}, bf16[2,4,4096]{2,1,0:T(4,128)(2,1)S(1)}, u32[]{:S(2)}, u32[]{:S(2)}) collective-permute-start(bf16[2,4,4096]{2,1,0:T(4,128)(2,1)} %bitcast.9), channel_id=1, source_target_pairs={{0,16},{2,18},{4,20},{6,22},{8,24},{10,26},{12,28},{14,30},{16,0},... | collective-permute-start | bytes 196616 | tf_op jit(solution)/shard_map/ppermute | solution.py:276
  3.1 0.1 collective-permute-start
  3.2 0.0 copy-start.1
  3.2 0.8 %copy-done.1 = bf16[1,2,4,4096]{3,2,1,0:T(4,128)(2,1)S(1)} copy-done((bf16[1,2,4,4096]{3,2,1,0:T(4,128)(2,1)S(1)}, bf16[1,2,4,4096]{3,2,1,0:T(4,128)(2,1)}, u32[]{:S(2)}) %copy-start.1) | copy-done | bytes 65560
  4.1 0.0 copy-start.2
  4.1 0.7 %copy-done.2 = s32[1,2,4]{2,1,0:T(2,128)S(1)} copy-done((s32[1,2,4]{2,1,0:T(2,128)S(1)}, s32[1,2,4]{2,1,0:T(2,128)}, u32[]{:S(2)}) %copy-start.2) | copy-done | bytes 56
  4.7 0.0 copy-start.3
  4.7 0.7 %copy-done.3 = s32[1,2,8]{2,1,0:T(2,128)S(1)} copy-done((s32[1,2,8]{2,1,0:T(2,128)S(1)}, s32[1,2,8]{2,1,0:T(2,128)}, u32[]{:S(2)}) %copy-start.3) | copy-done | bytes 88
  5.4 0.0 copy-start.4
  5.4 0.2 shard_map.64.refs_0_
  5.6 1.3 %collective-permute-start.3 = (bf16[32,4096]{1,0:T(8,128)(2,1)}, bf16[32,4096]{1,0:T(8,128)(2,1)S(1)}, u32[]{:S(2)}, u32[]{:S(2)}) collective-permute-start(bf16[32,4096]{1,0:T(8,128)(2,1)} %bitcast.7), channel_id=1, source_target_pairs={{0,1},{1,0},{2,3},{3,2},{4,5},{5,4},{6,7},{7,6},{8,9},{9,8},{10,11... | collective-permute-start | bytes 786440 | tf_op jit(solution)/shard_map/ppermute | solution.py:296
  7.5 0.0 collective-permute-done.slots_ref
  7.6 0.0 collective-permute-done.1.left_ref
  7.6 0.2 shard_map.65.part_ref.refs_2_
  7.8 1.4 %collective-permute-start.2 = (bf16[544,128]{1,0:T(8,128)(2,1)S(1)}, bf16[544,128]{1,0:T(8,128)(2,1)S(1)}, u32[]{:S(2)}, u32[]{:S(2)}) collective-permute-start(bf16[544,128]{1,0:T(8,128)(2,1)S(1)} %shard_map.65.part_ref.refs_2_), channel_id=1, source_target_pairs={{0,4},{2,10},{4,0},{6,14},{8,12},{10,2},{12,8},{14,6},{16,20},{18,... | collective-permute-start | bytes 417800 | tf_op jit(solution)/shard_map/ppermute | solution.py:276
  9.1 0.0 copy-done.4
  9.2 0.4 %collective-permute-start.4 = (s32[1,32]{1,0:T(1,128)S(1)}, s32[1,32]{1,0:T(1,128)S(1)}, u32[]{:S(2)}, u32[]{:S(2)}) collective-permute-start(s32[1,32]{1,0:T(1,128)S(1)} %compare_select_fusion.places_ref), channel_id=1, source_target_pairs={{0,1},{1,0},{2,3},{3,2},{4,5},{5,4},{6,7},{7,6},{8,9},{9,8},{10,11... | collective-permute-start | bytes 392 | tf_op jit(solution)/shard_map/ppermute | solution.py:296
  9.5 0.0 copy-done
  9.5 1.2 %shard_map.67.refs_0_ = bf16[1024,1024]{1,0:T(8,128)(2,1)S(1)} custom-call(s32[1,32]{1,0:T(1,128)S(1)} %compare_select_fusion.places_ref, bf16[32,4096]{1,0:T(8,128)(2,1)S(1)} %bitcast.8), custom_call_target="tpu_custom_call" | custom-call | flops 1300000000 | bytes 1000 | tf_op jit(solution)/shard_map/pallas_call | solution.py:135
  10.8 2.0 %collective-permute-done.4.places_ref = s32[1,32]{1,0:T(1,128)S(1)} collective-permute-done((s32[1,32]{1,0:T(1,128)S(1)}, s32[1,32]{1,0:T(1,128)S(1)}, u32[]{:S(2)}, u32[]{:S(2)}) %collective-permute-start.4) | collective-permute-done | bytes 160 | tf_op jit(solution)/shard_map/ppermute | solution.py:296
  12.7 0.0 collective-permute-done.2.part_ref.refs_2_
  12.7 0.0 collective-permute-done.3.values_ref
  12.8 1.0 %collective-permute-start.5 = (bf16[1088,128]{1,0:T(8,128)(2,1)S(1)}, bf16[1088,128]{1,0:T(8,128)(2,1)S(1)}, u32[]{:S(2)}, u32[]{:S(2)}) collective-permute-start(bf16[1088,128]{1,0:T(8,128)(2,1)S(1)} %shard_map.69), channel_id=1, source_target_pairs={{0,8},{2,6},{4,12},{6,2},{8,0},{10,14},{12,4},{14,10},{16,24},{18,... | collective-permute-start | bytes 835592 | tf_op jit(solution)/shard_map/ppermute | solution.py:276
  13.8 2.5 %collective-permute-start.6 = (bf16[544,128]{1,0:T(8,128)(2,1)S(1)}, bf16[544,128]{1,0:T(8,128)(2,1)S(1)}, u32[]{:S(2)}, u32[]{:S(2)}) collective-permute-start(bf16[544,128]{1,0:T(8,128)(2,1)S(1)} %shard_map.65.part_ref.refs_2_), channel_id=1, source_target_pairs={{0,2},{2,0},{4,6},{6,4},{8,10},{10,8},{12,14},{14,12},{16,18},{18,... | collective-permute-start | bytes 417800 | tf_op jit(solution)/shard_map/ppermute | solution.py:19
  16.3 0.0 collective-permute-start.7
  16.3 1.2 %shard_map.68.refs_1_ = bf16[1024,1024]{1,0:T(8,128)(2,1)S(1)} custom-call(s32[1,32]{1,0:T(1,128)S(1)} %collective-permute-done.4.places_ref, bf16[32,4096]{1,0:T(8,128)(2,1)S(1)} %collective-permute-done.3.values_ref), custom_call_target="tpu_custom_call" | custom-call | bytes 1000 | tf_op jit(solution)/shard_map/pallas_call | solution.py:135
  17.5 0.0 collective-permute-done.6.refs_3_
  17.6 1.8 %shard_map.70.refs_4_ = f32[512,1024]{1,0:T(8,128)} custom-call(bf16[1024,1024]{1,0:T(8,128)(2,1)S(1)} %shard_map.67.refs_0_, bf16[1024,1024]{1,0:T(8,128)(2,1)S(1)} %shard_map.68.refs_1_, bf16[544,128]{1,0:T(8,128)(2,1)S(1)} %shard_map.65.part_ref.refs_2_, bf16[544,128]{1,0:T(8,128)(2,1)S(1)} %collective-permute-done.6.refs_3_), custom_call_target="tpu_custom_call" | custom-call | flops 1000000 | bytes 1000 | tf_op jit(solution)/shard_map/pallas_call | solution.py:237
  19.4 0.0 collective-permute-done.7.refs_3_
  19.4 0.0 collective-permute-done.5.refs_2_.refs_4_
  19.4 1.9 %collective-permute-start.8 = (bf16[1088,128]{1,0:T(8,128)(2,1)S(1)}, bf16[1088,128]{1,0:T(8,128)(2,1)S(1)}, u32[]{:S(2)}, u32[]{:S(2)}) collective-permute-start(bf16[1088,128]{1,0:T(8,128)(2,1)S(1)} %collective-permute-done.5.refs_2_.refs_4_), channel_id=1, source_target_pairs={{0,2},{2,0},{4,6},{6,4},{8,10},{10,8},{12,14},{14,12},{16,18},{18,... | collective-permute-start | bytes 835592 | tf_op jit(solution)/shard_map/ppermute | solution.py:19
  21.3 1.8 %shard_map.71.refs_5_ = f32[512,1024]{1,0:T(8,128)} custom-call(bf16[1024,1024]{1,0:T(8,128)(2,1)S(1)} %shard_map.67.refs_0_, bf16[1024,1024]{1,0:T(8,128)(2,1)S(1)} %shard_map.68.refs_1_, bf16[1088,128]{1,0:T(8,128)(2,1)S(1)} %collective-permute-done.5.refs_2_.refs_4_, ...), custom_call_target="tpu_custom_call", output_to_operand_aliasing={{}: (4, {})} | custom-call | flops 1000000 | bytes 1000 | tf_op jit(solution)/shard_map/pallas_call | solution.py:237
  23.1 0.0 collective-permute-done.8.refs_3_
  23.1 2.7 %shard_map.72 = f32[512,1024]{1,0:T(8,128)} custom-call(bf16[1024,1024]{1,0:T(8,128)(2,1)S(1)} %shard_map.67.refs_0_, bf16[1024,1024]{1,0:T(8,128)(2,1)S(1)} %shard_map.68.refs_1_, bf16[544,128]{1,0:T(8,128)(2,1)S(1)} %collective-permute-done.2.part_ref.refs_2_, ...), custom_call_target="tpu_custom_call", output_to_operand_aliasing={{}: (5, {})} | custom-call | flops 1000000 | bytes 1000 | tf_op jit(solution)/shard_map/pallas_call | solution.py:237
  (3 shorter events, 0.0 us)
Async XLA Ops:
  0.0 9.5 %copy-start = (bf16[1,1,32,4096]{3,2,1,0:T(8,128)(2,1)S(1)}, bf16[1,1,32,4096]{3,2,1,0:T(8,128)(2,1)}, u32[]{:S(2)}) copy-start(bf16[1,1,32,4096]{3,2,1,0:T(8,128)(2,1)} %param.9) | copy-start | bytes 786436
  0.0 7.6 %collective-permute-start.1 = (bf16[2,4,4096]{2,1,0:T(4,128)(2,1)}, bf16[2,4,4096]{2,1,0:T(4,128)(2,1)S(1)}, u32[]{:S(2)}, u32[]{:S(2)}) collective-permute-start(bf16[2,4,4096]{2,1,0:T(4,128)(2,1)} %bitcast.9), channel_id=1, source_target_pairs={{0,16},{2,18},{4,20},{6,22},{8,24},{10,26},{12,28},{14,30},{16,0},... | collective-permute-start | bytes 196616 | tf_op jit(solution)/shard_map/ppermute | solution.py:276
  3.1 4.4 %collective-permute-start = (s32[2,4]{1,0:T(2,128)}, s32[2,4]{1,0:T(2,128)S(1)}, u32[]{:S(2)}, u32[]{:S(2)}) collective-permute-start(s32[2,4]{1,0:T(2,128)} %bitcast.11), channel_id=1, source_target_pairs={{0,16},{2,18},{4,20},{6,22},{8,24},{10,26},{12,28},{14,30},{16,0},... | collective-permute-start | bytes 104 | tf_op jit(solution)/shard_map/ppermute | solution.py:276
  3.2 0.8 %copy-start.1 = (bf16[1,2,4,4096]{3,2,1,0:T(4,128)(2,1)S(1)}, bf16[1,2,4,4096]{3,2,1,0:T(4,128)(2,1)}, u32[]{:S(2)}) copy-start(bf16[1,2,4,4096]{3,2,1,0:T(4,128)(2,1)} %param.6) | copy-start | bytes 196612
  4.1 0.7 %copy-start.2 = (s32[1,2,4]{2,1,0:T(2,128)S(1)}, s32[1,2,4]{2,1,0:T(2,128)}, u32[]{:S(2)}) copy-start(s32[1,2,4]{2,1,0:T(2,128)} %param.7) | copy-start | bytes 100
  4.7 0.7 %copy-start.3 = (s32[1,2,8]{2,1,0:T(2,128)S(1)}, s32[1,2,8]{2,1,0:T(2,128)}, u32[]{:S(2)}) copy-start(s32[1,2,8]{2,1,0:T(2,128)} %param.8) | copy-start | bytes 196
  5.4 3.7 %copy-start.4 = (s32[1,1,32]{2,1,0:T(1,128)S(1)}, s32[1,1,32]{2,1,0:T(1,128)}, u32[]{:S(2)}) copy-start(s32[1,1,32]{2,1,0:T(1,128)} %param.10) | copy-start | bytes 388
  5.6 7.1 %collective-permute-start.3 = (bf16[32,4096]{1,0:T(8,128)(2,1)}, bf16[32,4096]{1,0:T(8,128)(2,1)S(1)}, u32[]{:S(2)}, u32[]{:S(2)}) collective-permute-start(bf16[32,4096]{1,0:T(8,128)(2,1)} %bitcast.7), channel_id=1, source_target_pairs={{0,1},{1,0},{2,3},{3,2},{4,5},{5,4},{6,7},{7,6},{8,9},{9,8},{10,11... | collective-permute-start | bytes 786440 | tf_op jit(solution)/shard_map/ppermute | solution.py:296
  7.8 5.0 %collective-permute-start.2 = (bf16[544,128]{1,0:T(8,128)(2,1)S(1)}, bf16[544,128]{1,0:T(8,128)(2,1)S(1)}, u32[]{:S(2)}, u32[]{:S(2)}) collective-permute-start(bf16[544,128]{1,0:T(8,128)(2,1)S(1)} %shard_map.65.part_ref.refs_2_), channel_id=1, source_target_pairs={{0,4},{2,10},{4,0},{6,14},{8,12},{10,2},{12,8},{14,6},{16,20},{18,... | collective-permute-start | bytes 417800 | tf_op jit(solution)/shard_map/ppermute | solution.py:276
  9.2 3.6 %collective-permute-start.4 = (s32[1,32]{1,0:T(1,128)S(1)}, s32[1,32]{1,0:T(1,128)S(1)}, u32[]{:S(2)}, u32[]{:S(2)}) collective-permute-start(s32[1,32]{1,0:T(1,128)S(1)} %compare_select_fusion.places_ref), channel_id=1, source_target_pairs={{0,1},{1,0},{2,3},{3,2},{4,5},{5,4},{6,7},{7,6},{8,9},{9,8},{10,11... | collective-permute-start | bytes 392 | tf_op jit(solution)/shard_map/ppermute | solution.py:296
  12.8 6.6 %collective-permute-start.5 = (bf16[1088,128]{1,0:T(8,128)(2,1)S(1)}, bf16[1088,128]{1,0:T(8,128)(2,1)S(1)}, u32[]{:S(2)}, u32[]{:S(2)}) collective-permute-start(bf16[1088,128]{1,0:T(8,128)(2,1)S(1)} %shard_map.69), channel_id=1, source_target_pairs={{0,8},{2,6},{4,12},{6,2},{8,0},{10,14},{12,4},{14,10},{16,24},{18,... | collective-permute-start | bytes 835592 | tf_op jit(solution)/shard_map/ppermute | solution.py:276
  13.8 3.8 %collective-permute-start.6 = (bf16[544,128]{1,0:T(8,128)(2,1)S(1)}, bf16[544,128]{1,0:T(8,128)(2,1)S(1)}, u32[]{:S(2)}, u32[]{:S(2)}) collective-permute-start(bf16[544,128]{1,0:T(8,128)(2,1)S(1)} %shard_map.65.part_ref.refs_2_), channel_id=1, source_target_pairs={{0,2},{2,0},{4,6},{6,4},{8,10},{10,8},{12,14},{14,12},{16,18},{18,... | collective-permute-start | bytes 417800 | tf_op jit(solution)/shard_map/ppermute | solution.py:19
  16.3 3.0 %collective-permute-start.7 = (bf16[544,128]{1,0:T(8,128)(2,1)S(1)}, bf16[544,128]{1,0:T(8,128)(2,1)S(1)}, u32[]{:S(2)}, u32[]{:S(2)}) collective-permute-start(bf16[544,128]{1,0:T(8,128)(2,1)S(1)} %collective-permute-done.2.part_ref.refs_2_), channel_id=1, source_target_pairs={{0,2},{2,0},{4,6},{6,4},{8,10},{10,8},{12,14},{14,12},{16,18},{18,... | collective-permute-start | bytes 417800 | tf_op jit(solution)/shard_map/ppermute | solution.py:19
  19.4 3.7 %collective-permute-start.8 = (bf16[1088,128]{1,0:T(8,128)(2,1)S(1)}, bf16[1088,128]{1,0:T(8,128)(2,1)S(1)}, u32[]{:S(2)}, u32[]{:S(2)}) collective-permute-start(bf16[1088,128]{1,0:T(8,128)(2,1)S(1)} %collective-permute-done.5.refs_2_.refs_4_), channel_id=1, source_target_pairs={{0,2},{2,0},{4,6},{6,4},{8,10},{10,8},{12,14},{14,12},{16,18},{18,... | collective-permute-start | bytes 835592 | tf_op jit(solution)/shard_map/ppermute | solution.py:19

commit v5 on v4

--- a/solution.py
+++ b/solution.py
@@ -146,15 +146,18 @@
 def place_left(parcels, row, tiles, pairs, dense_ref, names_ref):
     half = (lax.broadcasted_iota(jnp.int32, (16, LANES), 1) // (LANES // 2)).astype(jnp.float32)
     body = tiles * pairs * 64
-    for i, (parcel, start) in enumerate(parcels):
-        names_ref[i * META : i * META + META, :] = parcel[pl.ds(start + body, META), :].astype(jnp.float32)
+    rows = [parcel[pl.ds(start + body, META), :].astype(jnp.float32) for parcel, start in parcels]
+    if tiles > 2:
+        for i, row_names in enumerate(rows):
+            names_ref[i * META : i * META + META, :] = row_names
 
     def one(m):
         names = []
         for i, (parcel, start) in enumerate(parcels):
             for p in range(pairs):
                 at = m * pairs + p
-                name = jnp.broadcast_to(names_ref[pl.ds(i * META + at, 1), :], (16, LANES))
+                name = names_ref[pl.ds(i * META + at, 1), :] if tiles > 2 else rows[i][at : at + 1, :]
+                name = jnp.broadcast_to(name, (16, LANES))
                 turned = pltpu.roll(name, LANES // 2, 1)
                 names.append((parcel, start + at * 64, (name - half).astype(jnp.bfloat16), (turned - half).astype(jnp.bfloat16)))
         plain, turned = [], []

time: 26 us -> 26 us (level)
  no operation moved by 1% of the time
where the time goes in v5:
time: 26 us; the launch traced here: 25.8 us
  starting transfers between devices  11.7 us (45%)
  Pallas kernels  9.04 us (35%)
  local copies, waits for them, and re-layouts  2.21 us (8%)
  waiting for transfers between devices  2.05 us (8%)
  between operations  0.76 us (3%)
    pallas_call x3, Pallas kernels, product(): pl.pallas_call(functools.partial(product_kernel, tiles, pairs, jobs, len(...  6.26 us
    ppermute x4, starting transfers between devices, by_core(): lax.ppermute(x, 'row', [(i, i ^ (one if i % 2 else zero)) for i in range(...  5.59 us
    ppermute x3, starting transfers between devices, swapped(): return lax.ppermute(x, 'row', [(i, i ^ mask) for i in range(peers)])  4.49 us
    pallas_call x2, Pallas kernels, dense_right(): pl.pallas_call(right_kernel, out_shape=jax.ShapeDtypeStruct((KB * side, B...  2.37 us
    unnamed x10, local copies, waits for them, and re-layouts  2.21 us
    ppermute x2, waiting for transfers between devices, from_col(): lax.ppermute(x, 'col', [(i, (i + by) % cols) for i in range(cols)])  2.01 us
    ppermute x2, starting transfers between devices, from_col(): lax.ppermute(x, 'col', [(i, (i + by) % cols) for i in range(cols)])  1.66 us
  transfers between devices with their start and end apart: 9, of which 1 were waited for; matrix products, arithmetic and copies ran while one was open for 0% of the time, Pallas kernels for 25%

profile of v5, /device:TPU:1, one launch (start us, length us, event | category | flops | bytes accessed | tf_op | source)
XLA Modules:
  0.0 25.8 jit_solution(10561475886399208433)
XLA Ops:
  0.0 0.0 copy-start
  0.0 3.1 %collective-permute-start.1 = (bf16[2,4,4096]{2,1,0:T(4,128)(2,1)}, bf16[2,4,4096]{2,1,0:T(4,128)(2,1)S(1)}, u32[]{:S(2)}, u32[]{:S(2)}) collective-permute-start(bf16[2,4,4096]{2,1,0:T(4,128)(2,1)} %bitcast.9), channel_id=1, source_target_pairs={{0,16},{2,18},{4,20},{6,22},{8,24},{10,26},{12,28},{14,30},{16,0},... | collective-permute-start | bytes 196616 | tf_op jit(solution)/shard_map/ppermute | solution.py:279
  3.1 0.1 collective-permute-start
  3.2 0.0 copy-start.1
  3.2 0.8 %copy-done.1 = bf16[1,2,4,4096]{3,2,1,0:T(4,128)(2,1)S(1)} copy-done((bf16[1,2,4,4096]{3,2,1,0:T(4,128)(2,1)S(1)}, bf16[1,2,4,4096]{3,2,1,0:T(4,128)(2,1)}, u32[]{:S(2)}) %copy-start.1) | copy-done | bytes 65560
  4.1 0.0 copy-start.2
  4.1 0.7 %copy-done.2 = s32[1,2,4]{2,1,0:T(2,128)S(1)} copy-done((s32[1,2,4]{2,1,0:T(2,128)S(1)}, s32[1,2,4]{2,1,0:T(2,128)}, u32[]{:S(2)}) %copy-start.2) | copy-done | bytes 56
  4.7 0.0 copy-start.3
  4.7 0.7 %copy-done.3 = s32[1,2,8]{2,1,0:T(2,128)S(1)} copy-done((s32[1,2,8]{2,1,0:T(2,128)S(1)}, s32[1,2,8]{2,1,0:T(2,128)}, u32[]{:S(2)}) %copy-start.3) | copy-done | bytes 88
  5.4 0.0 copy-start.4
  5.4 0.2 shard_map.64.refs_0_
  5.6 1.3 %collective-permute-start.3 = (bf16[32,4096]{1,0:T(8,128)(2,1)}, bf16[32,4096]{1,0:T(8,128)(2,1)S(1)}, u32[]{:S(2)}, u32[]{:S(2)}) collective-permute-start(bf16[32,4096]{1,0:T(8,128)(2,1)} %bitcast.7), channel_id=1, source_target_pairs={{0,1},{1,0},{2,3},{3,2},{4,5},{5,4},{6,7},{7,6},{8,9},{9,8},{10,11... | collective-permute-start | bytes 786440 | tf_op jit(solution)/shard_map/ppermute | solution.py:299
  7.5 0.0 collective-permute-done.slots_ref
  7.6 0.0 collective-permute-done.1.left_ref
  7.6 0.2 shard_map.65.part_ref.refs_2_
  7.8 1.4 %collective-permute-start.2 = (bf16[544,128]{1,0:T(8,128)(2,1)S(1)}, bf16[544,128]{1,0:T(8,128)(2,1)S(1)}, u32[]{:S(2)}, u32[]{:S(2)}) collective-permute-start(bf16[544,128]{1,0:T(8,128)(2,1)S(1)} %shard_map.65.part_ref.refs_2_), channel_id=1, source_target_pairs={{0,4},{2,10},{4,0},{6,14},{8,12},{10,2},{12,8},{14,6},{16,20},{18,... | collective-permute-start | bytes 417800 | tf_op jit(solution)/shard_map/ppermute | solution.py:279
  9.1 0.0 copy-done.4
  9.2 0.4 %collective-permute-start.4 = (s32[1,32]{1,0:T(1,128)S(1)}, s32[1,32]{1,0:T(1,128)S(1)}, u32[]{:S(2)}, u32[]{:S(2)}) collective-permute-start(s32[1,32]{1,0:T(1,128)S(1)} %compare_select_fusion.places_ref), channel_id=1, source_target_pairs={{0,1},{1,0},{2,3},{3,2},{4,5},{5,4},{6,7},{7,6},{8,9},{9,8},{10,11... | collective-permute-start | bytes 392 | tf_op jit(solution)/shard_map/ppermute | solution.py:299
  9.5 0.0 copy-done
  9.5 1.2 %shard_map.67.refs_0_ = bf16[1024,1024]{1,0:T(8,128)(2,1)S(1)} custom-call(s32[1,32]{1,0:T(1,128)S(1)} %compare_select_fusion.places_ref, bf16[32,4096]{1,0:T(8,128)(2,1)S(1)} %bitcast.8), custom_call_target="tpu_custom_call" | custom-call | flops 1300000000 | bytes 1000 | tf_op jit(solution)/shard_map/pallas_call | solution.py:135
  10.7 2.0 %collective-permute-done.4.places_ref = s32[1,32]{1,0:T(1,128)S(1)} collective-permute-done((s32[1,32]{1,0:T(1,128)S(1)}, s32[1,32]{1,0:T(1,128)S(1)}, u32[]{:S(2)}, u32[]{:S(2)}) %collective-permute-start.4) | collective-permute-done | bytes 160 | tf_op jit(solution)/shard_map/ppermute | solution.py:299
  12.7 0.0 collective-permute-done.2.part_ref.refs_2_
  12.7 0.0 collective-permute-done.3.values_ref
  12.8 1.0 %collective-permute-start.5 = (bf16[1088,128]{1,0:T(8,128)(2,1)S(1)}, bf16[1088,128]{1,0:T(8,128)(2,1)S(1)}, u32[]{:S(2)}, u32[]{:S(2)}) collective-permute-start(bf16[1088,128]{1,0:T(8,128)(2,1)S(1)} %shard_map.69), channel_id=1, source_target_pairs={{0,8},{2,6},{4,12},{6,2},{8,0},{10,14},{12,4},{14,10},{16,24},{18,... | collective-permute-start | bytes 835592 | tf_op jit(solution)/shard_map/ppermute | solution.py:279
  13.8 2.5 %collective-permute-start.6 = (bf16[544,128]{1,0:T(8,128)(2,1)S(1)}, bf16[544,128]{1,0:T(8,128)(2,1)S(1)}, u32[]{:S(2)}, u32[]{:S(2)}) collective-permute-start(bf16[544,128]{1,0:T(8,128)(2,1)S(1)} %shard_map.65.part_ref.refs_2_), channel_id=1, source_target_pairs={{0,2},{2,0},{4,6},{6,4},{8,10},{10,8},{12,14},{14,12},{16,18},{18,... | collective-permute-start | bytes 417800 | tf_op jit(solution)/shard_map/ppermute | solution.py:19
  16.3 0.0 collective-permute-start.7
  16.3 1.2 %shard_map.68.refs_1_ = bf16[1024,1024]{1,0:T(8,128)(2,1)S(1)} custom-call(s32[1,32]{1,0:T(1,128)S(1)} %collective-permute-done.4.places_ref, bf16[32,4096]{1,0:T(8,128)(2,1)S(1)} %collective-permute-done.3.values_ref), custom_call_target="tpu_custom_call" | custom-call | bytes 1000 | tf_op jit(solution)/shard_map/pallas_call | solution.py:135
  17.5 0.0 collective-permute-done.6.refs_3_
  17.6 1.8 %shard_map.70.refs_4_ = f32[512,1024]{1,0:T(8,128)} custom-call(bf16[1024,1024]{1,0:T(8,128)(2,1)S(1)} %shard_map.67.refs_0_, bf16[1024,1024]{1,0:T(8,128)(2,1)S(1)} %shard_map.68.refs_1_, bf16[544,128]{1,0:T(8,128)(2,1)S(1)} %shard_map.65.part_ref.refs_2_, bf16[544,128]{1,0:T(8,128)(2,1)S(1)} %collective-permute-done.6.refs_3_), custom_call_target="tpu_custom_call" | custom-call | flops 1000000 | bytes 1000 | tf_op jit(solution)/shard_map/pallas_call | solution.py:240
  19.4 0.0 collective-permute-done.7.refs_3_
  19.4 0.0 collective-permute-done.5.refs_2_.refs_4_
  19.4 1.9 %collective-permute-start.8 = (bf16[1088,128]{1,0:T(8,128)(2,1)S(1)}, bf16[1088,128]{1,0:T(8,128)(2,1)S(1)}, u32[]{:S(2)}, u32[]{:S(2)}) collective-permute-start(bf16[1088,128]{1,0:T(8,128)(2,1)S(1)} %collective-permute-done.5.refs_2_.refs_4_), channel_id=1, source_target_pairs={{0,2},{2,0},{4,6},{6,4},{8,10},{10,8},{12,14},{14,12},{16,18},{18,... | collective-permute-start | bytes 835592 | tf_op jit(solution)/shard_map/ppermute | solution.py:19
  21.3 1.8 %shard_map.71.refs_5_ = f32[512,1024]{1,0:T(8,128)} custom-call(bf16[1024,1024]{1,0:T(8,128)(2,1)S(1)} %shard_map.67.refs_0_, bf16[1024,1024]{1,0:T(8,128)(2,1)S(1)} %shard_map.68.refs_1_, bf16[1088,128]{1,0:T(8,128)(2,1)S(1)} %collective-permute-done.5.refs_2_.refs_4_, ...), custom_call_target="tpu_custom_call", output_to_operand_aliasing={{}: (4, {})} | custom-call | flops 1000000 | bytes 1000 | tf_op jit(solution)/shard_map/pallas_call | solution.py:240
  23.1 0.0 collective-permute-done.8.refs_3_
  23.1 2.7 %shard_map.72 = f32[512,1024]{1,0:T(8,128)} custom-call(bf16[1024,1024]{1,0:T(8,128)(2,1)S(1)} %shard_map.67.refs_0_, bf16[1024,1024]{1,0:T(8,128)(2,1)S(1)} %shard_map.68.refs_1_, bf16[544,128]{1,0:T(8,128)(2,1)S(1)} %collective-permute-done.2.part_ref.refs_2_, ...), custom_call_target="tpu_custom_call", output_to_operand_aliasing={{}: (5, {})} | custom-call | flops 1000000 | bytes 1000 | tf_op jit(solution)/shard_map/pallas_call | solution.py:240
  (3 shorter events, 0.0 us)
Async XLA Ops:
  0.0 9.5 %copy-start = (bf16[1,1,32,4096]{3,2,1,0:T(8,128)(2,1)S(1)}, bf16[1,1,32,4096]{3,2,1,0:T(8,128)(2,1)}, u32[]{:S(2)}) copy-start(bf16[1,1,32,4096]{3,2,1,0:T(8,128)(2,1)} %param.9) | copy-start | bytes 786436
  0.0 7.6 %collective-permute-start.1 = (bf16[2,4,4096]{2,1,0:T(4,128)(2,1)}, bf16[2,4,4096]{2,1,0:T(4,128)(2,1)S(1)}, u32[]{:S(2)}, u32[]{:S(2)}) collective-permute-start(bf16[2,4,4096]{2,1,0:T(4,128)(2,1)} %bitcast.9), channel_id=1, source_target_pairs={{0,16},{2,18},{4,20},{6,22},{8,24},{10,26},{12,28},{14,30},{16,0},... | collective-permute-start | bytes 196616 | tf_op jit(solution)/shard_map/ppermute | solution.py:279
  3.1 4.4 %collective-permute-start = (s32[2,4]{1,0:T(2,128)}, s32[2,4]{1,0:T(2,128)S(1)}, u32[]{:S(2)}, u32[]{:S(2)}) collective-permute-start(s32[2,4]{1,0:T(2,128)} %bitcast.11), channel_id=1, source_target_pairs={{0,16},{2,18},{4,20},{6,22},{8,24},{10,26},{12,28},{14,30},{16,0},... | collective-permute-start | bytes 104 | tf_op jit(solution)/shard_map/ppermute | solution.py:279
  3.2 0.8 %copy-start.1 = (bf16[1,2,4,4096]{3,2,1,0:T(4,128)(2,1)S(1)}, bf16[1,2,4,4096]{3,2,1,0:T(4,128)(2,1)}, u32[]{:S(2)}) copy-start(bf16[1,2,4,4096]{3,2,1,0:T(4,128)(2,1)} %param.6) | copy-start | bytes 196612
  4.1 0.7 %copy-start.2 = (s32[1,2,4]{2,1,0:T(2,128)S(1)}, s32[1,2,4]{2,1,0:T(2,128)}, u32[]{:S(2)}) copy-start(s32[1,2,4]{2,1,0:T(2,128)} %param.7) | copy-start | bytes 100
  4.7 0.7 %copy-start.3 = (s32[1,2,8]{2,1,0:T(2,128)S(1)}, s32[1,2,8]{2,1,0:T(2,128)}, u32[]{:S(2)}) copy-start(s32[1,2,8]{2,1,0:T(2,128)} %param.8) | copy-start | bytes 196
  5.4 3.7 %copy-start.4 = (s32[1,1,32]{2,1,0:T(1,128)S(1)}, s32[1,1,32]{2,1,0:T(1,128)}, u32[]{:S(2)}) copy-start(s32[1,1,32]{2,1,0:T(1,128)} %param.10) | copy-start | bytes 388
  5.6 7.1 %collective-permute-start.3 = (bf16[32,4096]{1,0:T(8,128)(2,1)}, bf16[32,4096]{1,0:T(8,128)(2,1)S(1)}, u32[]{:S(2)}, u32[]{:S(2)}) collective-permute-start(bf16[32,4096]{1,0:T(8,128)(2,1)} %bitcast.7), channel_id=1, source_target_pairs={{0,1},{1,0},{2,3},{3,2},{4,5},{5,4},{6,7},{7,6},{8,9},{9,8},{10,11... | collective-permute-start | bytes 786440 | tf_op jit(solution)/shard_map/ppermute | solution.py:299
  7.8 5.0 %collective-permute-start.2 = (bf16[544,128]{1,0:T(8,128)(2,1)S(1)}, bf16[544,128]{1,0:T(8,128)(2,1)S(1)}, u32[]{:S(2)}, u32[]{:S(2)}) collective-permute-start(bf16[544,128]{1,0:T(8,128)(2,1)S(1)} %shard_map.65.part_ref.refs_2_), channel_id=1, source_target_pairs={{0,4},{2,10},{4,0},{6,14},{8,12},{10,2},{12,8},{14,6},{16,20},{18,... | collective-permute-start | bytes 417800 | tf_op jit(solution)/shard_map/ppermute | solution.py:279
  9.2 3.6 %collective-permute-start.4 = (s32[1,32]{1,0:T(1,128)S(1)}, s32[1,32]{1,0:T(1,128)S(1)}, u32[]{:S(2)}, u32[]{:S(2)}) collective-permute-start(s32[1,32]{1,0:T(1,128)S(1)} %compare_select_fusion.places_ref), channel_id=1, source_target_pairs={{0,1},{1,0},{2,3},{3,2},{4,5},{5,4},{6,7},{7,6},{8,9},{9,8},{10,11... | collective-permute-start | bytes 392 | tf_op jit(solution)/shard_map/ppermute | solution.py:299
  12.8 6.6 %collective-permute-start.5 = (bf16[1088,128]{1,0:T(8,128)(2,1)S(1)}, bf16[1088,128]{1,0:T(8,128)(2,1)S(1)}, u32[]{:S(2)}, u32[]{:S(2)}) collective-permute-start(bf16[1088,128]{1,0:T(8,128)(2,1)S(1)} %shard_map.69), channel_id=1, source_target_pairs={{0,8},{2,6},{4,12},{6,2},{8,0},{10,14},{12,4},{14,10},{16,24},{18,... | collective-permute-start | bytes 835592 | tf_op jit(solution)/shard_map/ppermute | solution.py:279
  13.8 3.8 %collective-permute-start.6 = (bf16[544,128]{1,0:T(8,128)(2,1)S(1)}, bf16[544,128]{1,0:T(8,128)(2,1)S(1)}, u32[]{:S(2)}, u32[]{:S(2)}) collective-permute-start(bf16[544,128]{1,0:T(8,128)(2,1)S(1)} %shard_map.65.part_ref.refs_2_), channel_id=1, source_target_pairs={{0,2},{2,0},{4,6},{6,4},{8,10},{10,8},{12,14},{14,12},{16,18},{18,... | collective-permute-start | bytes 417800 | tf_op jit(solution)/shard_map/ppermute | solution.py:19
  16.3 3.0 %collective-permute-start.7 = (bf16[544,128]{1,0:T(8,128)(2,1)S(1)}, bf16[544,128]{1,0:T(8,128)(2,1)S(1)}, u32[]{:S(2)}, u32[]{:S(2)}) collective-permute-start(bf16[544,128]{1,0:T(8,128)(2,1)S(1)} %collective-permute-done.2.part_ref.refs_2_), channel_id=1, source_target_pairs={{0,2},{2,0},{4,6},{6,4},{8,10},{10,8},{12,14},{14,12},{16,18},{18,... | collective-permute-start | bytes 417800 | tf_op jit(solution)/shard_map/ppermute | solution.py:19
  19.4 3.7 %collective-permute-start.8 = (bf16[1088,128]{1,0:T(8,128)(2,1)S(1)}, bf16[1088,128]{1,0:T(8,128)(2,1)S(1)}, u32[]{:S(2)}, u32[]{:S(2)}) collective-permute-start(bf16[1088,128]{1,0:T(8,128)(2,1)S(1)} %collective-permute-done.5.refs_2_.refs_4_), channel_id=1, source_target_pairs={{0,2},{2,0},{4,6},{6,4},{8,10},{10,8},{12,14},{14,12},{16,18},{18,... | collective-permute-start | bytes 835592 | tf_op jit(solution)/shard_map/ppermute | solution.py:19
